TPU v7x, 32 devices: a whole 2x2x4 slice. The times are simulated.
32 devices in a mesh: groups: 2 (over y), ctx: 4 (over z), fsdp: 2 (over x), dp: 2 (over core).
Axes of the slice: x: 2, y: 2, z: 4, core: 2. Of those that a mesh axis runs over, the one named last changes fastest.
Arguments:
- query_in: bfloat16 [8, 512, 1024], P(('groups', 'fsdp', 'dp'), 'ctx'), parts along dimension 0, may hold values from -11 to 11
- key_in: bfloat16 [8, 512, 1024], P(('groups', 'fsdp', 'dp'), 'ctx'), parts along dimension 0, may hold values from -11 to 11
- value_in: bfloat16 [8, 512, 1024], P(('groups', 'fsdp', 'dp'), 'ctx'), parts along dimension 0, may hold values from -6 to 6
- utt_lengths: int32 [8], P(('groups', 'fsdp', 'dp')), parts along dimension 0, may hold values from 128 to 512, as said below
- frames_in: bfloat16 [8, 512, 1536], P(('groups', 'fsdp', 'dp'), 'ctx'), parts along dimension 0, may hold values from -6 to 6
- out_weight: bfloat16 [1024, 1536], P(None, 'fsdp'), may hold values from -1.5 to 1.5
- conv_kernel: float32 [31, 1536], P(None, 'fsdp'), may hold values from -1 to 1
- conv_bias: float32 [1536], P('fsdp'), may hold values from -3 to 3
- ln_gain: float32 [1536], P('fsdp'), may hold values from 0.1 to 1.9
- cotangent: bfloat16 [8, 512, 1536], P(('groups', 'fsdp', 'dp'), 'ctx'), parts along dimension 0, may hold values from -6 to 6
Outputs:
- block_out: bfloat16 [8, 512, 1536], P(('groups', 'fsdp', 'dp'), 'ctx'), parts along dimension 0
- hidden_grad: bfloat16 [8, 512, 1536], P(('groups', 'fsdp', 'dp'), 'ctx'), parts along dimension 0
- grad_kernel: float32 [62, 1536], P('groups', 'fsdp'), parts along dimension 0
- grad_bias: float32 [3072], P(('groups', 'fsdp')), parts along dimension 0
- grad_gain: float32 [3072], P(('groups', 'fsdp')), parts along dimension 0
There are 2 independent parts, one for each index of `groups`. A program takes and returns all parts, laid end to end along the dimension named above; an argument that names none is the same for every part. Nothing has to cross between parts.
Inputs may be any that keep to these rules, and one draw needn't show every extreme that they name: `utt_lengths`: in every group one utterance is full, of 512 valid frames.
All inputs are finite; a program needn't handle non-finite values.
Results may differ from a plain program's by a relative error of at most 0.019.
Values may be sent and summed in bfloat16 or wider, within the bound.
A program may use at most 64 MiB of HBM per device.

v0:
```python
import math

import jax
import jax.numpy as jnp
from jax import lax
from jax.sharding import PartitionSpec as P

HD = 64
TAPS = 31


NEG_FILL = -1e30


def extended(block, sides, width):
    for axis, dim in sides:
        count = lax.axis_size(axis)
        forward = [(i, i + 1) for i in range(count - 1)]
        backward = [(target, source) for source, target in forward]
        low = lax.ppermute(
            lax.slice_in_dim(block, block.shape[dim] - width, None, axis=dim), axis, forward
        )
        high = lax.ppermute(lax.slice_in_dim(block, 0, width, axis=dim), axis, backward)
        block = jnp.concatenate([low, block, high], axis=dim)
    return block


def absorb_block(state, query_heads, key_heads, value_heads, key_start, valid_len):
    run_max, run_sum, summed = state
    scores = jnp.einsum(
        "qhd,khd->qhk", query_heads, key_heads, preferred_element_type=jnp.float32
    ) * (1.0 / math.sqrt(HD))
    usable = key_start + jnp.arange(key_heads.shape[0]) < valid_len
    scores = jnp.where(usable, scores, NEG_FILL)
    new_max = jnp.maximum(run_max, jnp.max(scores, axis=-1))
    rescale = jnp.exp(run_max - new_max)
    weights = jnp.where(usable, jnp.exp(scores - new_max[..., None]), 0.0)
    run_sum = run_sum * rescale + jnp.sum(weights, axis=-1)
    summed = summed * rescale[..., None] + jnp.einsum(
        "qhk,khd->qhd",
        weights.astype(jnp.bfloat16),
        value_heads,
        preferred_element_type=jnp.float32,
    )
    return (new_max, run_sum, summed)


def normalize(block):
    as_float = block.astype(jnp.float32)
    average = jnp.mean(as_float, axis=-1, keepdims=True)
    centered = as_float - average
    variance = jnp.mean(centered * centered, axis=-1, keepdims=True)
    inv_scale = lax.rsqrt(variance + 1e-05)
    return (centered * inv_scale, inv_scale)


def convolve(conv_in, kernel_all, bias_all, out_rows):
    pre_act = bias_all + jnp.zeros((out_rows, conv_in.shape[1]), jnp.float32)
    for tap_index in range(TAPS):
        pre_act = pre_act + kernel_all[tap_index] * conv_in[tap_index : tap_index + out_rows]
    return pre_act


def live_of(positions, valid_len):
    return ((positions >= 0) & (positions < valid_len)).astype(jnp.float32)[:, None]


def shards(
    query_in,
    key_in,
    value_in,
    utt_lengths,
    frames_in,
    out_weight,
    conv_kernel,
    conv_bias,
    ln_gain,
    cotangent,
):
    row_count = query_in.shape[1]
    feat_width = query_in.shape[2]
    head_count = feat_width // HD
    valid_len = utt_lengths[0]
    ctx_count = lax.axis_size("ctx")
    row_offset = lax.axis_index("ctx") * row_count
    half_taps = TAPS // 2
    query_heads = query_in[0].reshape(row_count, head_count, HD)
    start_state = (
        jnp.full((row_count, head_count), NEG_FILL, jnp.float32),
        jnp.zeros((row_count, head_count), jnp.float32),
        jnp.zeros((row_count, head_count, HD), jnp.float32),
    )
    state = start_state
    first_row = jnp.int32(0)
    key_part = lax.all_gather(key_in, "ctx", axis=1, tiled=True)
    value_part = lax.all_gather(value_in, "ctx", axis=1, tiled=True)
    piece_rows = key_part.shape[1]
    block_len = math.gcd(piece_rows, 512)
    for block_start in range(0, piece_rows, block_len):
        key_heads = key_part[0, block_start : block_start + block_len].reshape(
            block_len, head_count, HD
        )
        value_heads = value_part[0, block_start : block_start + block_len].reshape(
            block_len, head_count, HD
        )
        state = absorb_block(
            state, query_heads, key_heads, value_heads, first_row + block_start, valid_len
        )
    run_max, run_sum, summed = state
    attended = (summed / run_sum[..., None]).reshape(row_count, feat_width).astype(jnp.bfloat16)
    projected = jnp.dot(
        attended,
        lax.all_gather(out_weight, "fsdp", axis=1, tiled=True),
        preferred_element_type=jnp.float32,
    )
    hidden = (frames_in[0].astype(jnp.float32) + projected).astype(jnp.bfloat16)
    kernel_all, bias_all, gain_all = (
        lax.all_gather(conv_kernel, "fsdp", axis=1, tiled=True),
        lax.all_gather(conv_bias, "fsdp", axis=0, tiled=True),
        lax.all_gather(ln_gain, "fsdp", axis=0, tiled=True),
    )
    grad_in = cotangent[0].astype(jnp.float32)
    live_mask = live_of(row_offset + jnp.arange(row_count), valid_len)
    widened = extended(hidden, (("ctx", 0),), half_taps)
    normed_ext, inv_ext = normalize(widened)
    conv_in = (
        live_of(row_offset - half_taps + jnp.arange(row_count + 2 * half_taps), valid_len)
        * normed_ext
        * gain_all
    )
    pre_act = convolve(conv_in, kernel_all, bias_all, row_count)
    gate_val = jax.nn.sigmoid(pre_act)
    grad_pre = grad_in * live_mask * gate_val * (1.0 + pre_act * (1.0 - gate_val))
    grad_wide = extended(grad_pre.astype(jnp.bfloat16), (("ctx", 0),), half_taps).astype(
        grad_pre.dtype
    )
    normed = normed_ext[half_taps : half_taps + row_count]
    inv_scale = inv_ext[half_taps : half_taps + row_count]
    block_out = (hidden.astype(jnp.float32) + live_mask * pre_act * gate_val).astype(jnp.bfloat16)
    grad_conv = jnp.zeros((row_count, grad_pre.shape[1]), jnp.float32)
    kernel_rows = []
    for tap_index in range(TAPS):
        back = 2 * half_taps - tap_index
        grad_conv = grad_conv + kernel_all[tap_index] * grad_wide[back : back + row_count]
        kernel_rows.append(jnp.sum(grad_pre * conv_in[tap_index : tap_index + row_count], axis=0))
    grad_conv = live_mask * grad_conv
    grad_hat = grad_conv * gain_all
    first_mean = jnp.mean(grad_hat, axis=-1, keepdims=True)
    second_mean = jnp.mean(grad_hat * normed, axis=-1, keepdims=True)
    hidden_grad = (grad_in + (grad_hat - first_mean - normed * second_mean) * inv_scale).astype(
        jnp.bfloat16
    )
    factor = 1.0 / math.sqrt(lax.axis_size("fsdp") * lax.axis_size("dp") * row_count * ctx_count)
    kernel_term = jnp.stack(kernel_rows) * factor
    bias_term = (jnp.sum(grad_pre, axis=0) * factor)[None]
    gain_term = (jnp.sum(grad_conv * normed, axis=0) * factor)[None]
    shares = (
        lax.psum_scatter(
            kernel_term.astype(jnp.bfloat16), "fsdp", scatter_dimension=1, tiled=True
        ).astype(jnp.float32),
        lax.psum_scatter(
            bias_term.astype(jnp.bfloat16), "fsdp", scatter_dimension=1, tiled=True
        ).astype(jnp.float32),
        lax.psum_scatter(
            gain_term.astype(jnp.bfloat16), "fsdp", scatter_dimension=1, tiled=True
        ).astype(jnp.float32),
    )
    totals = lax.psum((shares[0], shares[1], shares[2]), ("ctx", "dp"))
    return (block_out[None], hidden_grad[None], totals[0], totals[1][0], totals[2][0])


def solution(mesh):
    in_specs = (
        P(("groups", "fsdp", "dp"), "ctx", None),
        P(("groups", "fsdp", "dp"), "ctx", None),
        P(("groups", "fsdp", "dp"), "ctx", None),
        P(("groups", "fsdp", "dp")),
        P(("groups", "fsdp", "dp"), "ctx", None),
        P(None, "fsdp"),
        P(None, "fsdp"),
        P("fsdp"),
        P("fsdp"),
        P(("groups", "fsdp", "dp"), "ctx", None),
    )
    out_specs = (
        P(("groups", "fsdp", "dp"), "ctx", None),
        P(("groups", "fsdp", "dp"), "ctx", None),
        P("groups", "fsdp"),
        P(("groups", "fsdp")),
        P(("groups", "fsdp")),
    )
    return jax.shard_map(shards, mesh=mesh, in_specs=in_specs, out_specs=out_specs, check_vma=False)
```

profile of v0, /device:TPU:0, one launch (start us, length us, event | category | flops | bytes accessed | tf_op | source)
XLA Modules:
  0.0 231.5 jit_solution(14485959095688557060)
XLA Ops:
  7.2 0.7 all-gather.6.cloned.1.call-update
  7.9 0.7 all-gather.8.cloned.1.call-update
  8.7 0.7 all-gather.10.cloned.1.call-update
  10.1 1.1 copy.24
  11.2 6.7 %all_gather.22 = f32[31,1536]{1,0:T(8,128)S(1)} all-gather(f32[31,768]{1,0:T(8,128)} %param.16), channel_id=1, replica_groups=mesh['groups'=2,'ctx'=4,'fsdp'=2,'dp'=2] {'fsdp'}, dimensions={1}, use_global_device_ids=true | all-gather | bytes 285696 | tf_op jit(solution)/shard_map/all_gather | solution.py:118
  18.4 21.8 %all-gather.6.cloned.1.call-done = bf16[1,512,1024]{2,1,0:T(8,128)(2,1)} async-done(((bf16[1,128,1024]{2,1,0:T(8,128)(2,1)}), bf16[1,512,1024]{2,1,0:T(8,128)(2,1)}) %all-gather.6.cloned.1.call-update) | async-done | bytes 1048592 | tf_op jit(solution)/shard_map/all_gather | solution.py:95
  40.2 1.5 copy.23
  41.7 27.5 %all-gather.8.cloned.1.call-done = bf16[1,512,1024]{2,1,0:T(8,128)(2,1)} async-done(((bf16[1,128,1024]{2,1,0:T(8,128)(2,1)}), bf16[1,512,1024]{2,1,0:T(8,128)(2,1)}) %all-gather.8.cloned.1.call-update) | async-done | bytes 1048592 | tf_op jit(solution)/shard_map/all_gather | solution.py:96
  69.3 1.5 copy.25
  70.8 1.1 bitcast_reduce_fusion
  71.9 1.2 fusion.2
  73.1 1.5 fusion.20
  74.6 40.7 %all-gather.10.cloned.1.call-done = bf16[1024,1536]{1,0:T(8,128)(2,1)} async-done(((bf16[1024,768]{1,0:T(8,128)(2,1)}), bf16[1024,1536]{1,0:T(8,128)(2,1)}) %all-gather.10.cloned.1.call-update) | async-done | bytes 3145744 | tf_op jit(solution)/shard_map/all_gather | solution.py:113
  115.3 2.5 %fusion.4 = bf16[128,1536]{1,0:T(8,128)(2,1)S(1)} fusion(bf16[128,1024]{0,1:T(8,128)(2,1)S(1)} %bitcast.62, bf16[1024,1536]{1,0:T(8,128)(2,1)} %all-gather.10.cloned.1.call-done, bf16[1,128,1536]{2,1,0:T(8,128)(2,1)S(1)} %copy-done.1), kind=kOutput, calls=%fused_computation.8 | convolution fusion | flops 403243008 | bytes 4194304 | tf_op jit(solution)/shard_map/dot_general | solution.py:111
  117.8 3.4 %collective-permute-start = (bf16[15,1536]{1,0:T(8,128)(2,1)S(1)}, bf16[15,1536]{1,0:T(8,128)(2,1)S(1)}, u32[]{:S(2)}, u32[]{:S(2)}) collective-permute-start(bf16[15,1536]{1,0:T(8,128)(2,1)S(1)} %get-tuple-element.82), channel_id=1, source_target_pairs={{0,4},{4,8},{8,12},{1,5},{5,9},{9,13},{2,6},{6,10},{10,14},{3,7},{... | collective-permute-start | bytes 138248 | tf_op jit(solution)/shard_map/ppermute | solution.py:20
  121.2 1.3 collective-permute-start.1
  122.5 4.3 %all-gather.1 = f32[2,1,768]{2,1,0:T(1,128)S(1)} all-gather(f32[1,1,768]{2,1,0:T(1,128)S(1)} %reshape.114), channel_id=1, replica_groups=mesh['groups'=2,'ctx'=4,'fsdp'=2,'dp'=2] {'fsdp'}, dimensions={0}, use_global_device_ids=true | all-gather | bytes 9216 | tf_op jit(solution)/shard_map/all_gather | solution.py:120
  126.9 4.3 %all-gather = f32[2,1,768]{2,1,0:T(1,128)S(1)} all-gather(f32[1,1,768]{2,1,0:T(1,128)S(1)} %reshape.112), channel_id=1, replica_groups=mesh['groups'=2,'ctx'=4,'fsdp'=2,'dp'=2] {'fsdp'}, dimensions={0}, use_global_device_ids=true | all-gather | bytes 9216 | tf_op jit(solution)/shard_map/all_gather | solution.py:119
  131.6 0.3 fusion.23
  131.9 0.3 fusion.15
  132.3 6.3 %multiply_reduce_fusion.1 = (f32[1536]{0:T(1024)S(1)}, f32[1536]{0:T(1024)S(1)}, f32[1536]{0:T(1024)S(1)}, f32[1536]{0:T(1024)S(1)}, f32[1536]{0:T(1024)S(1)}, /...) fusion(f32[158,1536]{1,0:T(8,128)S(1)} %get-tuple-element.79, ...), kind=kLoop, calls=%fused_computation.90 | loop fusion | flops 21206016 | bytes 26653184 | tf_op jit(solution)/shard_map/reduce_sum | solution.py:145
  138.6 2.1 multiply_reduce_fusion.19
  140.8 4.5 %collective-permute-start.2 = (bf16[15,1536]{1,0:T(8,128)(2,1)S(1)}, bf16[15,1536]{1,0:T(8,128)(2,1)S(1)}, u32[]{:S(2)}, u32[]{:S(2)}) collective-permute-start(bf16[15,1536]{1,0:T(8,128)(2,1)S(1)} %get-tuple-element.80), channel_id=1, source_target_pairs={{0,4},{4,8},{8,12},{1,5},{5,9},{9,13},{2,6},{6,10},{10,14},{3,7},{... | collective-permute-start | bytes 138248 | tf_op jit(solution)/shard_map/ppermute | solution.py:20
  145.3 1.3 collective-permute-start.3
  146.6 1.0 reshape_bitcast_fusion.1
  147.9 1.7 fusion.59
  149.6 0.7 stack.100
  150.3 0.7 stack.101
  151.0 0.7 stack.102
  151.7 0.7 stack.103
  152.4 0.7 stack.104
  153.1 0.7 stack.105
  153.8 0.7 stack.106
  154.5 0.7 stack.107
  155.2 0.7 stack.108
  155.9 0.7 stack.96
  156.6 0.7 stack.97
  157.3 0.7 stack.98
  158.0 0.7 stack.99
  159.4 6.1 %multiply_reduce_fusion = (f32[1536]{0:T(1024)S(1)}, f32[128]{0:T(128)S(1)}, f32[128]{0:T(128)S(1)}, f32[128,1536]{1,0:T(8,128)S(1)}) fusion(f32[158,1536]{1,0:T(8,128)S(1)} %get-tuple-element.78, f32[1536]{0:T(1024)S(1)} %reshape.115, f32[158,1536]{1,0:T(8,128)S(1)} %maximum_convert_fusion, f32[1536]{0:T(1024)S(1)} %get-tuple-element.41, ...), kind=kLoop, calls=%fused_computation.89 | loop fusion | flops 13367552 | bytes 26156544 | tf_op jit(solution)/shard_map/reduce_sum | solution.py:156
  165.6 1.0 reshape_bitcast_fusion
  166.6 0.7 multiply_convert_fusion
  167.4 1.0 copy.29
  168.5 1.1 fusion.58
  169.5 11.5 %reduce-scatter.12.cloned.1.call-done = bf16[768,1]{1,0:T(8,128)(2,1)} async-done(((bf16[1536,1]{1,0:T(8,128)(2,1)}), bf16[768,1]{1,0:T(8,128)(2,1)}) %reduce-scatter.12.cloned.1.call-update) | async-done | bytes 1552
  181.0 1.0 copy.31
  182.1 11.6 %reduce-scatter.8.cloned.1.call-done = bf16[31,768]{1,0:T(8,128)(2,1)} async-done(((bf16[31,1536]{1,0:T(8,128)(2,1)}), bf16[31,768]{1,0:T(8,128)(2,1)}) %reduce-scatter.8.cloned.1.call-update) | async-done | bytes 47632 | tf_op jit(solution)/shard_map/reduce_scatter | solution.py:158
  193.7 31.0 %all-reduce.2 = (f32[31,768]{1,0:T(8,128)}, f32[768]{0:T(1024)}, f32[768]{0:T(1024)}) all-reduce(bf16[31,768]{1,0:T(8,128)(2,1)} %reduce-scatter.8.cloned.1.call-done, f32[768]{0:T(1024)S(1)} %get-tuple-element.91, f32[768]{0:T(1024)S(1)} %get-tuple-element.90), channel_id=1, replica_groups=mesh['groups'=2,'ctx'=4,'fsdp'=2,'dp'=2] {'ctx','dp'}, use_global_device_ids=true, to_apply=%region_38.39 | all-reduce | flops 25344 | bytes 155136 | tf_op jit(solution)/shard_map/psum | solution.py:168
  (71 shorter events, 2.1 us)
Async XLA Ops:
  7.2 33.1 %all-gather.6.cloned.1.call-start = ((), (), s32[]{:S(2)}) async-start(), calls=%async_computation.3 | async-start | bytes 1310720 | tf_op jit(solution)/shard_map/all_gather | solution.py:95
  7.9 61.4 %all-gather.8.cloned.1.call-start = ((), (), s32[]{:S(2)}) async-start(), calls=%async_computation.4 | async-start | bytes 1310720 | tf_op jit(solution)/shard_map/all_gather | solution.py:96
  8.6 106.6 %all-gather.10.cloned.1.call-start = ((), (), s32[]{:S(2)}) async-start(), calls=%async_computation.5 | async-start | bytes 4718592 | tf_op jit(solution)/shard_map/all_gather | solution.py:113
  9.4 158.0 %reduce-scatter.10.cloned.1.call-start = ((), (), s32[]{:S(2)}) async-start(), calls=%async_computation.7 | async-start | bytes 589824
  73.1 42.2 %copy-start.1 = (bf16[1,128,1536]{2,1,0:T(8,128)(2,1)S(1)}, bf16[1,128,1536]{2,1,0:T(8,128)(2,1)}, u32[]{:S(2)}) copy-start(bf16[1,128,1536]{2,1,0:T(8,128)(2,1)} %param.14) | copy-start | bytes 1179652
  74.5 48.0 %copy-start.5 = (f32[768]{0:T(1024)S(1)}, f32[768]{0:T(1024)}, u32[]{:S(2)}) copy-start(f32[768]{0:T(1024)} %param.18) | copy-start | bytes 9220
  74.5 52.4 %copy-start.6 = (f32[768]{0:T(1024)S(1)}, f32[768]{0:T(1024)}, u32[]{:S(2)}) copy-start(f32[768]{0:T(1024)} %param.17) | copy-start | bytes 9220
  74.6 57.7 %copy-start = (bf16[1,128,1536]{2,1,0:T(8,128)(2,1)S(1)}, bf16[1,128,1536]{2,1,0:T(8,128)(2,1)}, u32[]{:S(2)}) copy-start(bf16[1,128,1536]{2,1,0:T(8,128)(2,1)} %param.19) | copy-start | bytes 1179652
  117.8 13.5 %collective-permute-start = (bf16[15,1536]{1,0:T(8,128)(2,1)S(1)}, bf16[15,1536]{1,0:T(8,128)(2,1)S(1)}, u32[]{:S(2)}, u32[]{:S(2)}) collective-permute-start(bf16[15,1536]{1,0:T(8,128)(2,1)S(1)} %get-tuple-element.82), channel_id=1, source_target_pairs={{0,4},{4,8},{8,12},{1,5},{5,9},{9,13},{2,6},{6,10},{10,14},{3,7},{... | collective-permute-start | bytes 138248 | tf_op jit(solution)/shard_map/ppermute | solution.py:20
  121.2 10.1 %collective-permute-start.1 = (bf16[15,1536]{1,0:T(8,128)(2,1)S(1)}, bf16[15,1536]{1,0:T(8,128)(2,1)S(1)}, u32[]{:S(2)}, u32[]{:S(2)}) collective-permute-start(bf16[15,1536]{1,0:T(8,128)(2,1)S(1)} %get-tuple-element.83), channel_id=1, source_target_pairs={{4,0},{8,4},{12,8},{5,1},{9,5},{13,9},{6,2},{10,6},{14,10},{7,3},{... | collective-permute-start | bytes 138248 | tf_op jit(solution)/shard_map/ppermute | solution.py:23
  122.5 16.1 %copy-start.2 = (f32[128]{0:T(128)}, f32[128]{0:T(128)S(1)}, u32[]{:S(2)}) copy-start(f32[128]{0:T(128)S(1)} %and_convert_fusion.1) | copy-start | bytes 1540
  131.9 6.7 %copy-start.3 = (f32[158]{0:T(256)}, f32[158]{0:T(256)S(1)}, u32[]{:S(2)}) copy-start(f32[158]{0:T(256)S(1)} %add_rsqrt_fusion) | copy-start | bytes 1900
  140.8 18.5 %collective-permute-start.2 = (bf16[15,1536]{1,0:T(8,128)(2,1)S(1)}, bf16[15,1536]{1,0:T(8,128)(2,1)S(1)}, u32[]{:S(2)}, u32[]{:S(2)}) collective-permute-start(bf16[15,1536]{1,0:T(8,128)(2,1)S(1)} %get-tuple-element.80), channel_id=1, source_target_pairs={{0,4},{4,8},{8,12},{1,5},{5,9},{9,13},{2,6},{6,10},{10,14},{3,7},{... | collective-permute-start | bytes 138248 | tf_op jit(solution)/shard_map/ppermute | solution.py:20
  145.3 14.0 %collective-permute-start.3 = (bf16[15,1536]{1,0:T(8,128)(2,1)S(1)}, bf16[15,1536]{1,0:T(8,128)(2,1)S(1)}, u32[]{:S(2)}, u32[]{:S(2)}) collective-permute-start(bf16[15,1536]{1,0:T(8,128)(2,1)S(1)} %get-tuple-element.81), channel_id=1, source_target_pairs={{4,0},{8,4},{12,8},{5,1},{9,5},{13,9},{6,2},{10,6},{14,10},{7,3},{... | collective-permute-start | bytes 138248 | tf_op jit(solution)/shard_map/ppermute | solution.py:23
  147.7 33.4 %reduce-scatter.12.cloned.1.call-start = ((), (), s32[]{:S(2)}) async-start(), calls=%async_computation.8 | async-start | bytes 589824
  159.4 7.9 %copy-start.4 = (f32[158]{0:T(256)S(1)}, f32[158]{0:T(256)}, u32[]{:S(2)}) copy-start(f32[158]{0:T(256)} %copy-done.3) | copy-start | bytes 1900
  166.6 27.1 %reduce-scatter.8.cloned.1.call-start = ((), (), s32[]{:S(2)}) async-start(), calls=%async_computation.6 | async-start | bytes 147456 | tf_op jit(solution)/shard_map/reduce_scatter | solution.py:158
Sparse Core Ops, SparseCore 0:
  9.6 30.6 all-gather.5
  41.8 27.4 all-gather.7
  70.8 44.4 all-gather.9
  147.8 14.2 reduce-scatter.9
  166.7 14.2 reduce-scatter.11
  183.6 9.9 reduce-scatter.7
where the time goes:
time: 233 us; the launch traced here: 232 us
  waiting for transfers between devices  115 us (49%)
  blocking collectives  46.4 us (20%)
  other arithmetic  20.3 us (9%)
  local copies, waits for them, and re-layouts  18.4 us (8%)
  between operations  15.2 us (7%)
  starting transfers between devices  10.9 us (5%)
  matrix products  5.07 us (2%)
    all_gather x1, waiting for transfers between devices, shards(): lax.all_gather(out_weight, 'fsdp', axis=1, tiled=True)  40.7 us
    psum x1, blocking collectives, shards(): totals = lax.psum((shares[0], shares[1], shares[2]), ('ctx', 'dp'))  31 us
    all_gather x1, waiting for transfers between devices, shards(): value_part = lax.all_gather(value_in, 'ctx', axis=1, tiled=True)  27.5 us
    all_gather x1, waiting for transfers between devices, shards(): key_part = lax.all_gather(key_in, 'ctx', axis=1, tiled=True)  21.8 us
    unnamed x8, waiting for transfers between devices  13.6 us
    reduce_scatter x1, waiting for transfers between devices, shards(): lax.psum_scatter(kernel_term.astype(jnp.bfloat16), 'fsdp', scatter_dimens...  11.6 us
    another operation x32, local copies, waits for them, and re-layouts, shards(): kernel_term = jnp.stack(kernel_rows) * factor  9.55 us
    reduce_sum x2, other arithmetic, shards(): jnp.sum(grad_pre * conv_in[tap_index:tap_index + row_count], axis=0)  8.42 us
  transfers between devices with their start and end apart: 10, of which 5 were waited for; matrix products, arithmetic and copies ran while one was open for 14% of the time, Pallas kernels for 0%

commit v1 on v0

--- a/solution.py
+++ b/solution.py
@@ -1,9 +1,16 @@
+import functools
 import math
 
 import jax
 import jax.numpy as jnp
 from jax import lax
+from jax.experimental import pallas as pl
+from jax.experimental.pallas import tpu as pltpu
 from jax.sharding import PartitionSpec as P
+
+MESH = pl.DeviceIdType.MESH
+LANES = 128
+EDGE = 16
 
 HD = 64
 TAPS = 31
@@ -169,6 +176,598 @@
     return (block_out[None], hidden_grad[None], totals[0], totals[1][0], totals[2][0])
 
 
+def fused_kernel(
+    nz,
+    q_ref,
+    k_ref,
+    v_ref,
+    len_ref,
+    frames_ref,
+    weight_ref,
+    taps_ref,
+    bias_ref,
+    gain_ref,
+    cot_ref,
+    block_ref,
+    hgrad_ref,
+    gk_ref,
+    gb_ref,
+    gg_ref,
+    qkv,
+    osend,
+    obuf,
+    wbuf,
+    frames,
+    cot,
+    pk,
+    pb,
+    pg,
+    kp,
+    proj,
+    hid,
+    nl,
+    invs,
+    live,
+    gext,
+    hsend,
+    hrecv,
+    gsend,
+    grecv,
+    ghat,
+    sums,
+    mf,
+    mb,
+    abuf,
+    rs1,
+    bsend,
+    bbuf,
+    zbuf,
+    tot,
+    local_sem,
+    qkv_local,
+    qkv_ss,
+    qkv_rs,
+    o_local,
+    o_ss,
+    o_rs,
+    w_ss,
+    w_rs,
+    wf_ss,
+    wf_rs,
+    p_ss,
+    p_rs,
+    h_ss,
+    h_rs,
+    g_ss,
+    g_rs,
+    r_ss,
+    r_rs,
+    z_ss,
+    z_rs,
+):
+    f32, bf16 = jnp.float32, jnp.bfloat16
+    gi = lax.axis_index("groups")
+    z = lax.axis_index("ctx")
+    x = lax.axis_index("fsdp")
+    c = lax.axis_index("dp")
+    rows = q_ref.shape[1]
+    parts = qkv.shape[0]
+    part_cols = nz * LANES
+    tiles = proj.shape[0]
+    half = tiles // 2
+    quarter = half // 2
+    wrows = wbuf.shape[1] // parts // 2
+    feats = tiles * LANES
+
+    def at_z(zz):
+        return (gi, zz, x, c)
+
+    x_peer = (gi, z, 1 - x, c)
+    sibling = (gi, z, x, 1 - c)
+
+    def remote(src, dst, ss, rs, dev):
+        return pltpu.make_async_remote_copy(
+            src_ref=src, dst_ref=dst, send_sem=ss, recv_sem=rs, device_id=dev, device_id_type=MESH
+        )
+
+    in_refs = (q_ref, k_ref, v_ref)
+
+    def qkv_src(p, a, zz):
+        start = pl.multiple_of(p * part_cols + zz * LANES, LANES)
+        return in_refs[a].at[0, :, pl.ds(start, LANES)]
+
+    def qkv_dst(p, a, zz):
+        return qkv.at[p, a, pl.ds(pl.multiple_of(zz * rows, rows), rows), :]
+
+    def qkv_send(p, a, off):
+        dest = lax.rem(z + off, nz)
+        return remote(
+            qkv_src(p, a, dest),
+            qkv_dst(p, a, z),
+            qkv_ss.at[p, a, off - 1],
+            qkv_rs.at[p, a, off - 1],
+            at_z(dest),
+        )
+
+    def qkv_own(p, a):
+        return pltpu.make_async_copy(qkv_src(p, a, z), qkv_dst(p, a, z), qkv_local.at[p, a])
+
+    def o_send(p, off):
+        dest = lax.rem(z + off, nz)
+        return remote(
+            osend.at[p, off - 1],
+            obuf.at[p, :, pl.ds(pl.multiple_of(z * LANES, LANES), LANES)],
+            o_ss.at[p, off - 1],
+            o_rs.at[p, off - 1],
+            at_z(dest),
+        )
+
+    def w_rows(p, core):
+        return pl.ds(pl.multiple_of((p * 2 + core) * wrows, wrows), wrows)
+
+    def w_send(p):
+        return remote(
+            weight_ref.at[w_rows(p, c), :],
+            wbuf.at[x, w_rows(p, c), :],
+            w_ss.at[p],
+            w_rs.at[p],
+            x_peer,
+        )
+
+    def w_forward(p):
+        return remote(
+            wbuf.at[1 - x, w_rows(p, c), :],
+            wbuf.at[1 - x, w_rows(p, c), :],
+            wf_ss.at[p],
+            wf_rs.at[p],
+            sibling,
+        )
+
+    def p_send(i):
+        src = (taps_ref, bias_ref, gain_ref)[i]
+        dst = (pk, pb, pg)[i]
+        return remote(src, dst.at[x], p_ss.at[i], p_rs.at[i], x_peer)
+
+    local_copies = (
+        pltpu.make_async_copy(weight_ref, wbuf.at[x], local_sem.at[0]),
+        pltpu.make_async_copy(frames_ref.at[0], frames, local_sem.at[1]),
+        pltpu.make_async_copy(cot_ref.at[0], cot, local_sem.at[2]),
+    )
+
+    barrier = pltpu.get_barrier_semaphore()
+    partners = [at_z(lax.rem(z + off, nz)) for off in range(1, nz)] + [x_peer, sibling]
+    for dev in partners:
+        pl.semaphore_signal(barrier, inc=1, device_id=dev, device_id_type=MESH)
+    pl.semaphore_wait(barrier, len(partners))
+
+    for p in range(parts):
+        for a in range(3):
+            for off in range(1, nz):
+                qkv_send(p, a, off).start()
+        w_send(p).start()
+        if p == 0:
+            for i in range(3):
+                p_send(i).start()
+        for a in range(3):
+            qkv_own(p, a).start()
+    for copy in local_copies:
+        copy.start()
+    pk[x] = taps_ref[...]
+    pb[x] = bias_ref[...]
+    pg[x] = gain_ref[...]
+
+    valid_len = len_ref[0]
+    keys = nz * rows
+    key_fill = jnp.where(
+        lax.broadcasted_iota(jnp.int32, (1, keys), 1) < valid_len, 0.0, NEG_FILL
+    ).astype(f32)
+    low_lanes = lax.broadcasted_iota(jnp.int32, (rows, LANES), 1) < HD
+    ext = rows + 2 * EDGE
+    positions = z * rows - EDGE + lax.broadcasted_iota(jnp.int32, (ext, LANES), 0)
+    live[...] = jnp.where((positions >= 0) & (positions < valid_len), 1.0, 0.0).astype(f32)
+
+    def attend(p, off):
+        zq = lax.rem(z + off, nz)
+        query = qkv[p, 0, pl.ds(pl.multiple_of(zq * rows, rows), rows), :]
+        pieces = []
+        for head in range(2):
+            keep = low_lanes if head == 0 else jnp.logical_not(low_lanes)
+            one = jnp.where(keep, query, jnp.zeros_like(query))
+            scores = lax.dot_general(
+                one, qkv[p, 1], (((1,), (1,)), ((), ())), preferred_element_type=f32
+            )
+            scores = scores + key_fill
+            top = jnp.max(scores, axis=1, keepdims=True)
+            weights = jnp.exp((scores - top) * (1.0 / math.sqrt(HD)))
+            total = jnp.sum(weights, axis=1, keepdims=True)
+            summed = jnp.dot(weights.astype(bf16), qkv[p, 2], preferred_element_type=f32)
+            pieces.append(summed / total)
+        return jnp.where(low_lanes, pieces[0], pieces[1]).astype(bf16)
+
+    def attend_part(p):
+        for a in range(3):
+            qkv_own(p, a).wait()
+            for off in range(1, nz):
+                qkv_send(p, a, off).wait_recv()
+
+        def one_chunk(i, carry):
+            osend[p, i] = attend(p, i + 1)
+            o_send(p, i + 1).start()
+            return carry
+
+        lax.fori_loop(0, nz - 1, one_chunk, 0)
+        obuf[p, :, pl.ds(pl.multiple_of(z * LANES, LANES), LANES)] = attend(p, 0)
+
+    def project(p):
+        for off in range(1, nz):
+            o_send(p, off).wait_recv()
+        w_forward(p).wait_recv()
+        attended = obuf[p]
+        for h in range(2):
+            block = wbuf[h, p * part_cols : (p + 1) * part_cols, :]
+            product = jnp.dot(attended, block, preferred_element_type=f32)
+            for t in range(half):
+                piece = product[:, t * LANES : (t + 1) * LANES]
+                if p == 0:
+                    proj[h * half + t] = piece
+                else:
+                    proj[h * half + t] += piece
+
+    attend_part(0)
+    for i in range(3):
+        p_send(i).wait_recv()
+    n_taps = pk.shape[1]
+    for h in range(2):
+        for t in range(half):
+            cols = slice(t * LANES, (t + 1) * LANES)
+            kp[h * half + t, 0:n_taps, :] = pk[h, :, cols] * pg[h, :, cols]
+            kp[h * half + t, n_taps : n_taps + 1, :] = pb[h, :, cols]
+    for p in range(1, parts):
+        w_send(p - 1).wait_recv()
+        w_forward(p - 1).start()
+        attend_part(p)
+    w_send(parts - 1).wait_recv()
+    w_forward(parts - 1).start()
+    for copy in local_copies:
+        copy.wait()
+    for p in range(parts):
+        project(p)
+
+    def lane_cols(t):
+        return pl.ds(pl.multiple_of(t * LANES, LANES), LANES)
+
+    def finish_hidden(t, carry):
+        value = (frames[:, lane_cols(t)].astype(f32) + proj[t]).astype(bf16)
+        hsend[0, t] = value[0:EDGE]
+        hsend[1, t] = value[rows - EDGE : rows]
+        hid[t, EDGE : EDGE + rows, :] = value.astype(f32)
+        return carry
+
+    lax.fori_loop(0, tiles, finish_hidden, 0)
+
+    def edge_copies(send, recv, ss, rs):
+        up = remote(send.at[0], recv.at[1], ss.at[0], rs.at[1], at_z(lax.rem(z + nz - 1, nz)))
+        down = remote(send.at[1], recv.at[0], ss.at[1], rs.at[0], at_z(lax.rem(z + 1, nz)))
+        return up, down
+
+    def edges_start(send, recv, ss, rs):
+        up, down = edge_copies(send, recv, ss, rs)
+
+        @pl.when(z > 0)
+        def _():
+            up.start()
+
+        @pl.when(z == 0)
+        def _():
+            recv[0] = jnp.zeros(recv.shape[1:], recv.dtype)
+
+        @pl.when(z < nz - 1)
+        def _():
+            down.start()
+
+        @pl.when(z == nz - 1)
+        def _():
+            recv[1] = jnp.zeros(recv.shape[1:], recv.dtype)
+
+    def edges_wait(send, recv, ss, rs):
+        up, down = edge_copies(send, recv, ss, rs)
+
+        @pl.when(z > 0)
+        def _():
+            up.wait_send()
+            down.wait_recv()
+
+        @pl.when(z < nz - 1)
+        def _():
+            down.wait_send()
+            up.wait_recv()
+
+    def norm_rows(start, count):
+        total = jnp.zeros((count, LANES), f32)
+        for t in range(tiles):
+            total = total + hid[t, start : start + count, :]
+        mean = jnp.sum(total, axis=1, keepdims=True) * (1.0 / feats)
+        total = jnp.zeros((count, LANES), f32)
+        for t in range(tiles):
+            centered = hid[t, start : start + count, :] - mean
+            total = total + centered * centered
+        inv = lax.rsqrt(jnp.sum(total, axis=1, keepdims=True) * (1.0 / feats) + 1e-05)
+        scale = live[start : start + count, :] * inv
+        for t in range(tiles):
+            nl[t, start : start + count, :] = (hid[t, start : start + count, :] - mean) * scale
+        return inv
+
+    edges_start(hsend, hrecv, h_ss, h_rs)
+    invs[...] = jnp.broadcast_to(norm_rows(EDGE, rows), (rows, LANES))
+    edges_wait(hsend, hrecv, h_ss, h_rs)
+    for t in range(tiles):
+        hid[t, 0:EDGE, :] = hrecv[0, t].astype(f32)
+        hid[t, EDGE + rows : ext, :] = hrecv[1, t].astype(f32)
+    norm_rows(0, EDGE)
+    norm_rows(EDGE + rows, EDGE)
+
+    def shifted_sum(acc, source, t, flip):
+        for r in range(8):
+            window = source[t, r : r + rows + 24, :]
+            for a in range(4):
+                shift = 8 * a + r
+                tap = n_taps - shift if flip else shift - 1
+                if shift > 0:
+                    acc = acc + kp[t, tap : tap + 1, :] * window[8 * a : 8 * a + rows]
+        return acc
+
+    def forward(t, carry):
+        start = jnp.broadcast_to(kp[t, n_taps : n_taps + 1, :], (rows, LANES))
+        pre = shifted_sum(start, nl, t, False)
+        alive = live[EDGE : EDGE + rows, :]
+        gate = 1.0 / (1.0 + jnp.exp(-pre))
+        hidden = hid[t, EDGE : EDGE + rows, :]
+        block_ref[:, lane_cols(t)] = (hidden + alive * pre * gate).astype(bf16)
+        grad_in = cot[:, lane_cols(t)].astype(f32)
+        grad_pre = grad_in * alive * gate * (1.0 + pre * (1.0 - gate))
+        gext[t, EDGE : EDGE + rows, :] = grad_pre
+        gsend[0, t] = grad_pre[0:EDGE].astype(bf16)
+        gsend[1, t] = grad_pre[rows - EDGE : rows].astype(bf16)
+        return carry
+
+    lax.fori_loop(0, tiles, forward, 0)
+    edges_start(gsend, grecv, g_ss, g_rs)
+
+    def tap_sums(t, carry):
+        grad_pre = gext[t, EDGE : EDGE + rows, :]
+        for r in range(8):
+            window = nl[t, r : r + rows + 24, :]
+            for a in range(4):
+                shift = 8 * a + r
+                if shift > 0:
+                    mf[t, shift - 1 : shift, :] = jnp.sum(
+                        grad_pre * window[8 * a : 8 * a + rows], axis=0, keepdims=True
+                    )
+        mf[t, n_taps : n_taps + 1, :] = jnp.sum(grad_pre, axis=0, keepdims=True)
+        mb[t] = mf[t].astype(bf16)
+        return carry
+
+    lax.fori_loop(0, tiles, tap_sums, 0)
+    to_x = remote(mb.at[pl.ds((1 - x) * half, half)], abuf, r_ss.at[0], r_rs.at[0], x_peer)
+    to_x.start()
+
+    edges_wait(gsend, grecv, g_ss, g_rs)
+    for t in range(tiles):
+        gext[t, 0:EDGE, :] = grecv[0, t].astype(f32)
+        gext[t, EDGE + rows : ext, :] = grecv[1, t].astype(f32)
+    sums[...] = jnp.zeros(sums.shape, f32)
+
+    def backward(t, carry):
+        acc = shifted_sum(jnp.zeros((rows, LANES), f32), gext, t, True)
+        acc = acc * live[EDGE : EDGE + rows, :]
+        ghat[t] = acc
+        sums[0] += acc
+        sums[1] += acc * nl[t, EDGE : EDGE + rows, :]
+        return carry
+
+    lax.fori_loop(0, half, backward, 0)
+
+    to_x.wait()
+    rs1[...] = mf[pl.ds(x * half, half)] + abuf[...].astype(f32)
+    bsend[...] = rs1[pl.ds((1 - c) * quarter, quarter)].astype(bf16)
+    to_core = remote(bsend, bbuf, r_ss.at[1], r_rs.at[1], sibling)
+    to_core.start()
+
+    lax.fori_loop(half, tiles, backward, 0)
+
+    to_core.wait()
+    zbuf[z] = (rs1[pl.ds(c * quarter, quarter)] + bbuf[...].astype(f32)).astype(bf16)
+
+    def z_send(off):
+        return remote(
+            zbuf.at[z],
+            zbuf.at[z],
+            z_ss.at[off - 1],
+            z_rs.at[off - 1],
+            at_z(lax.rem(z + off, nz)),
+        )
+
+    for off in range(1, nz):
+        z_send(off).start()
+
+    first_mean = jnp.sum(sums[0], axis=1, keepdims=True) * (1.0 / feats)
+    second_mean = jnp.sum(sums[1], axis=1, keepdims=True) * (1.0 / feats)
+
+    def finish_grad(t, carry):
+        inner = ghat[t] - first_mean - nl[t, EDGE : EDGE + rows, :] * second_mean
+        value = cot[:, lane_cols(t)].astype(f32) + inner * invs[...]
+        hgrad_ref[:, lane_cols(t)] = value.astype(bf16)
+        return carry
+
+    lax.fori_loop(0, tiles, finish_grad, 0)
+
+    for off in range(1, nz):
+        z_send(off).wait()
+    whole = zbuf[0].astype(f32)
+    for zz in range(1, nz):
+        whole = whole + zbuf[zz].astype(f32)
+    mine = pl.ds(c * quarter, quarter)
+    tot[mine] = whole
+    back = remote(tot.at[mine], tot.at[mine], r_ss.at[2], r_rs.at[2], sibling)
+    back.start()
+
+    for p in range(parts):
+        for off in range(1, nz):
+            for a in range(3):
+                qkv_send(p, a, off).wait_send()
+            o_send(p, off).wait_send()
+        w_send(p).wait_send()
+        w_forward(p).wait_send()
+    for i in range(3):
+        p_send(i).wait_send()
+
+    back.wait()
+    factor = 1.0 / math.sqrt(4 * rows * nz)
+    for t in range(half):
+        cols = slice(t * LANES, (t + 1) * LANES)
+        taps_sum = tot[t, 0:n_taps, :] * factor
+        gk_ref[:, cols] = taps_sum * gain_ref[:, cols]
+        gb_ref[:, cols] = tot[t, n_taps : n_taps + 1, :] * factor
+        gg_ref[:, cols] = jnp.sum(taps_sum * taps_ref[:, cols], axis=0, keepdims=True)
+
+
+def fused_shards(
+    query_in,
+    key_in,
+    value_in,
+    utt_lengths,
+    frames_in,
+    out_weight,
+    conv_kernel,
+    conv_bias,
+    ln_gain,
+    cotangent,
+):
+    f32, bf16 = jnp.float32, jnp.bfloat16
+    nz = lax.axis_size("ctx")
+    rows, width = query_in.shape[1:]
+    feats = frames_in.shape[2]
+    cols = out_weight.shape[1]
+    parts = width // (nz * LANES)
+    tiles = feats // LANES
+    half, quarter = tiles // 2, tiles // 4
+    ext = rows + 2 * EDGE
+    taps = conv_kernel.shape[0]
+    vmem, dma = pltpu.VMEM, pltpu.SemaphoreType.DMA
+    scratch = [
+        vmem((parts, 3, nz * rows, LANES), bf16),
+        vmem((parts, nz - 1, rows, LANES), bf16),
+        vmem((parts, rows, nz * LANES), bf16),
+        vmem((2, width, cols), bf16),
+        vmem((rows, feats), bf16),
+        vmem((rows, feats), bf16),
+        vmem((2, taps, cols), f32),
+        vmem((2, 1, cols), f32),
+        vmem((2, 1, cols), f32),
+        vmem((tiles, taps + 1, LANES), f32),
+        vmem((tiles, rows, LANES), f32),
+        vmem((tiles, ext, LANES), f32),
+        vmem((tiles, ext, LANES), f32),
+        vmem((rows, LANES), f32),
+        vmem((ext, LANES), f32),
+        vmem((tiles, ext, LANES), f32),
+        vmem((2, tiles, EDGE, LANES), bf16),
+        vmem((2, tiles, EDGE, LANES), bf16),
+        vmem((2, tiles, EDGE, LANES), bf16),
+        vmem((2, tiles, EDGE, LANES), bf16),
+        vmem((tiles, rows, LANES), f32),
+        vmem((2, rows, LANES), f32),
+        vmem((tiles, taps + 1, LANES), f32),
+        vmem((tiles, taps + 1, LANES), bf16),
+        vmem((half, taps + 1, LANES), bf16),
+        vmem((half, taps + 1, LANES), f32),
+        vmem((quarter, taps + 1, LANES), bf16),
+        vmem((quarter, taps + 1, LANES), bf16),
+        vmem((nz, quarter, taps + 1, LANES), bf16),
+        vmem((half, taps + 1, LANES), f32),
+        dma((3,)),
+        dma((parts, 3)),
+        dma((parts, 3, nz - 1)),
+        dma((parts, 3, nz - 1)),
+        dma((parts,)),
+        dma((parts, nz - 1)),
+        dma((parts, nz - 1)),
+        dma((parts,)),
+        dma((parts,)),
+        dma((parts,)),
+        dma((parts,)),
+        dma((3,)),
+        dma((3,)),
+        dma((2,)),
+        dma((2,)),
+        dma((2,)),
+        dma((2,)),
+        dma((3,)),
+        dma((3,)),
+        dma((nz - 1,)),
+        dma((nz - 1,)),
+    ]
+    here = pl.BlockSpec(memory_space=pltpu.VMEM)
+    there = pl.BlockSpec(memory_space=pl.ANY)
+    block_out, hidden_grad, grad_kernel, grad_bias, grad_gain = pl.pallas_call(
+        functools.partial(fused_kernel, nz),
+        out_shape=(
+            jax.ShapeDtypeStruct((rows, feats), bf16),
+            jax.ShapeDtypeStruct((rows, feats), bf16),
+            jax.ShapeDtypeStruct((taps, cols), f32),
+            jax.ShapeDtypeStruct((1, cols), f32),
+            jax.ShapeDtypeStruct((1, cols), f32),
+        ),
+        in_specs=[
+            there,
+            there,
+            there,
+            pl.BlockSpec(memory_space=pltpu.SMEM),
+            there,
+            there,
+            here,
+            here,
+            here,
+            there,
+        ],
+        out_specs=(here,) * 5,
+        scratch_shapes=scratch,
+        compiler_params=pltpu.CompilerParams(
+            collective_id=0, has_side_effects=True, vmem_limit_bytes=40 * 1024 * 1024
+        ),
+        name="conformer_window",
+    )(
+        query_in,
+        key_in,
+        value_in,
+        utt_lengths,
+        frames_in,
+        out_weight,
+        conv_kernel,
+        conv_bias[None],
+        ln_gain[None],
+        cotangent,
+    )
+    return (block_out[None], hidden_grad[None], grad_kernel, grad_bias[0], grad_gain[0])
+
+
+def shards_any(*args):
+    rows, width = args[0].shape[1:]
+    cols = args[5].shape[1]
+    nz = lax.axis_size("ctx")
+    fits = (
+        lax.axis_size("fsdp") == 2
+        and lax.axis_size("dp") == 2
+        and 2 <= nz
+        and rows % LANES == 0
+        and width % (nz * LANES) == 0
+        and cols % (2 * LANES) == 0
+        and nz <= 4
+        and args[0].shape[0] == 1
+    )
+    return fused_shards(*args) if fits else shards(*args)
+
+
 def solution(mesh):
     in_specs = (
         P(("groups", "fsdp", "dp"), "ctx", None),
@@ -189,4 +788,4 @@
         P(("groups", "fsdp")),
         P(("groups", "fsdp")),
     )
-    return jax.shard_map(shards, mesh=mesh, in_specs=in_specs, out_specs=out_specs, check_vma=False)
+    return jax.shard_map(shards_any, mesh=mesh, in_specs=in_specs, out_specs=out_specs, check_vma=False)

time: 233 us -> 63.3 us (0.27)
  waiting for transfers between devices: 115 us -> 0 us
  Pallas kernels: 0 us -> 49.7 us
  blocking collectives: 46.4 us -> 0 us
  other arithmetic: 20.3 us -> 1.21 us
  between operations: 15.2 us -> 1.3 us
  starting transfers between devices: 10.9 us -> 0 us
  local copies, waits for them, and re-layouts: 18.4 us -> 10.6 us
  matrix products: 5.07 us -> 0 us
    all_gather x3 -> x0, waiting for transfers between devices: 90.1 us -> none  [the longest x1 40.7 us: shards(): lax.all_gather(out_weight, 'fsdp', axis=1, tiled=True)]
    pallas_call x0 -> x1, Pallas kernels: none -> 49.7 us  [fused_shards(): pl.pallas_call(functools.partial(fused_kernel, nz), out_shape=(jax.ShapeD...]
    psum x1 -> x0, blocking collectives: 31 us -> none  [shards(): totals = lax.psum((shares[0], shares[1], shares[2]), ('ctx', 'dp'))]
    reduce_sum x6 -> x0, other arithmetic: 16.3 us -> none  [the longest x2 8.42 us: shards(): jnp.sum(grad_pre * conv_in[tap_index:tap_index + row_count], axis=0)]
    all_gather x3 -> x0, blocking collectives: 15.3 us -> none  [the longest x1 6.66 us: shards(): lax.all_gather(conv_kernel, 'fsdp', axis=1, tiled=True)]
    unnamed x8 -> x0, waiting for transfers between devices: 13.6 us -> none
    reduce_scatter x1 -> x0, waiting for transfers between devices: 11.6 us -> none  [shards(): lax.psum_scatter(kernel_term.astype(jnp.bfloat16), 'fsdp', scatter_dimens...]
    ppermute x4 -> x0, starting transfers between devices: 10.5 us -> none  [the longest x2 7.94 us: extended(): lax.ppermute(lax.slice_in_dim(block, block.shape[dim] - width, None, axis...]
  transfers between devices with their start and end apart: 10 -> 0, of which waited for: 5 -> 0; matrix products, arithmetic and copies ran while one was open for 14% -> 0% of each run, Pallas kernels for 0% -> 0%
where the time goes in v1:
time: 63.3 us; the launch traced here: 62.8 us
  Pallas kernels  49.7 us (79%)
  local copies, waits for them, and re-layouts  10.6 us (17%)
  between operations  1.3 us (2%)
  other arithmetic  1.21 us (2%)
    pallas_call x1, Pallas kernels, fused_shards(): pl.pallas_call(functools.partial(fused_kernel, nz), out_shape=(jax.ShapeD...  49.7 us
    unnamed x17, local copies, waits for them, and re-layouts  9.27 us

profile of v1, /device:TPU:0, one launch (start us, length us, event | category | flops | bytes accessed | tf_op | source)
XLA Modules:
  0.0 62.8 jit_solution(864762228770814994)
XLA Ops:
  1.3 0.7 %broadcast_in_dim.12.bias_ref = f32[1,768]{1,0:T(1,128)S(1)} reshape(f32[768]{0:T(1024)} %param.17) | data formatting | bytes 6144 | tf_op jit(solution)/shard_map/broadcast_in_dim | solution.py:747
  2.0 0.7 %broadcast_in_dim.13.gain_ref = f32[1,768]{1,0:T(1,128)S(1)} reshape(f32[768]{0:T(1024)} %param.18) | data formatting | bytes 6144 | tf_op jit(solution)/shard_map/broadcast_in_dim | solution.py:748
  2.7 0.0 copy-start
  2.7 1.4 %copy-done = bf16[1024,768]{1,0:T(8,128)(2,1)S(1)} copy-done((bf16[1024,768]{1,0:T(8,128)(2,1)S(1)}, bf16[1024,768]{1,0:T(8,128)(2,1)}, u32[]{:S(2)}) %copy-start) | copy-done | bytes 1572888
  4.1 0.0 copy-start.1
  4.1 1.0 %copy-done.1 = bf16[1,128,1536]{2,1,0:T(8,128)(2,1)S(1)} copy-done((bf16[1,128,1536]{2,1,0:T(8,128)(2,1)S(1)}, bf16[1,128,1536]{2,1,0:T(8,128)(2,1)}, u32[]{:S(2)}) %copy-start.1) | copy-done | bytes 393240
  5.1 0.0 copy-start.2
  5.1 1.0 %copy-done.2 = bf16[1,128,1536]{2,1,0:T(8,128)(2,1)S(1)} copy-done((bf16[1,128,1536]{2,1,0:T(8,128)(2,1)S(1)}, bf16[1,128,1536]{2,1,0:T(8,128)(2,1)}, u32[]{:S(2)}) %copy-start.2) | copy-done | bytes 393240
  6.1 0.0 copy-start.3
  6.1 0.9 %copy-done.3 = bf16[1,128,1024]{2,1,0:T(8,128)(2,1)S(1)} copy-done((bf16[1,128,1024]{2,1,0:T(8,128)(2,1)S(1)}, bf16[1,128,1024]{2,1,0:T(8,128)(2,1)}, u32[]{:S(2)}) %copy-start.3) | copy-done | bytes 262168
  7.0 0.0 copy-start.4
  7.0 0.9 %copy-done.4 = bf16[1,128,1024]{2,1,0:T(8,128)(2,1)S(1)} copy-done((bf16[1,128,1024]{2,1,0:T(8,128)(2,1)S(1)}, bf16[1,128,1024]{2,1,0:T(8,128)(2,1)}, u32[]{:S(2)}) %copy-start.4) | copy-done | bytes 262168
  8.0 0.0 copy-start.5
  8.0 0.9 %copy-done.5 = bf16[1,128,1024]{2,1,0:T(8,128)(2,1)S(1)} copy-done((bf16[1,128,1024]{2,1,0:T(8,128)(2,1)S(1)}, bf16[1,128,1024]{2,1,0:T(8,128)(2,1)}, u32[]{:S(2)}) %copy-start.5) | copy-done | bytes 262168
  8.9 0.0 copy-start.6
  8.9 0.9 %copy-done.6 = f32[31,768]{1,0:T(8,128)S(1)} copy-done((f32[31,768]{1,0:T(8,128)S(1)}, f32[31,768]{1,0:T(8,128)}, u32[]{:S(2)}) %copy-start.6) | copy-done | bytes 95256
  9.8 49.7 %conformer_window.1 = (bf16[128,1536]{1,0:T(8,128)(2,1)S(1)}, bf16[128,1536]{1,0:T(8,128)(2,1)S(1)}, f32[31,768]{1,0:T(8,128)S(1)}, f32[1,768]{1,0:T(1,128)S(1)}, f32[1,768]{1,0:T(1,128)S(1)}) custom-call(bf16[1,128,1024]{2,1,0:T(8,128)(2,1)S(1)} %copy-done.3, bf16[1,128,1024]{2,1,0:T(8,128)(2,1)S(1)} %copy-done.4, bf16[1,128,1024]{2,1,0:T(8,128)(2,1)S(1)} %copy-done.5, ...), custom_call_target="tpu_custom_call" | custom-call | tf_op jit(solution)/shard_map/conformer_window/pallas_call | solution.py:712
  59.5 0.6 reduce
  60.1 0.6 reduce.1
  60.7 0.7 %copy.19 = bf16[1,128,1536]{2,1,0:T(8,128)(2,1)} copy(bf16[1,128,1536]{2,1,0:T(8,128)(2,1)S(1)} %bitcast.3) | data formatting | bytes 786432
  61.4 0.7 %copy.20 = bf16[1,128,1536]{2,1,0:T(8,128)(2,1)} copy(bf16[1,128,1536]{2,1,0:T(8,128)(2,1)S(1)} %bitcast.2) | data formatting | bytes 786432
  62.2 0.6 %copy.21 = f32[31,768]{1,0:T(8,128)} copy(f32[31,768]{1,0:T(8,128)S(1)} %get-tuple-element.22) | data formatting | bytes 190464
Async XLA Ops:
  2.7 1.4 %copy-start = (bf16[1024,768]{1,0:T(8,128)(2,1)S(1)}, bf16[1024,768]{1,0:T(8,128)(2,1)}, u32[]{:S(2)}) copy-start(bf16[1024,768]{1,0:T(8,128)(2,1)} %weight_ref.1) | copy-start | bytes 4718596
  4.1 1.0 %copy-start.1 = (bf16[1,128,1536]{2,1,0:T(8,128)(2,1)S(1)}, bf16[1,128,1536]{2,1,0:T(8,128)(2,1)}, u32[]{:S(2)}) copy-start(bf16[1,128,1536]{2,1,0:T(8,128)(2,1)} %frames_ref.1) | copy-start | bytes 1179652
  5.1 1.0 %copy-start.2 = (bf16[1,128,1536]{2,1,0:T(8,128)(2,1)S(1)}, bf16[1,128,1536]{2,1,0:T(8,128)(2,1)}, u32[]{:S(2)}) copy-start(bf16[1,128,1536]{2,1,0:T(8,128)(2,1)} %cot_ref.1) | copy-start | bytes 1179652
  6.1 0.9 %copy-start.3 = (bf16[1,128,1024]{2,1,0:T(8,128)(2,1)S(1)}, bf16[1,128,1024]{2,1,0:T(8,128)(2,1)}, u32[]{:S(2)}) copy-start(bf16[1,128,1024]{2,1,0:T(8,128)(2,1)} %q_ref.1) | copy-start | bytes 786436
  7.0 0.9 %copy-start.4 = (bf16[1,128,1024]{2,1,0:T(8,128)(2,1)S(1)}, bf16[1,128,1024]{2,1,0:T(8,128)(2,1)}, u32[]{:S(2)}) copy-start(bf16[1,128,1024]{2,1,0:T(8,128)(2,1)} %k_ref.1) | copy-start | bytes 786436
  8.0 0.9 %copy-start.5 = (bf16[1,128,1024]{2,1,0:T(8,128)(2,1)S(1)}, bf16[1,128,1024]{2,1,0:T(8,128)(2,1)}, u32[]{:S(2)}) copy-start(bf16[1,128,1024]{2,1,0:T(8,128)(2,1)} %v_ref.1) | copy-start | bytes 786436
  8.9 0.9 %copy-start.6 = (f32[31,768]{1,0:T(8,128)S(1)}, f32[31,768]{1,0:T(8,128)}, u32[]{:S(2)}) copy-start(f32[31,768]{1,0:T(8,128)} %taps_ref.1) | copy-start | bytes 285700

commit v2 on v1

--- a/solution.py
+++ b/solution.py
@@ -11,6 +11,7 @@
 MESH = pl.DeviceIdType.MESH
 LANES = 128
 EDGE = 16
+VMEM_GRANT = 60 * 1024 * 1024
 
 HD = 64
 TAPS = 31
@@ -188,8 +189,8 @@
     bias_ref,
     gain_ref,
     cot_ref,
-    block_ref,
-    hgrad_ref,
+    block_out,
+    hgrad_out,
     gk_ref,
     gb_ref,
     gg_ref,
@@ -223,6 +224,8 @@
     bbuf,
     zbuf,
     tot,
+    block_ref,
+    hgrad_ref,
     local_sem,
     qkv_local,
     qkv_ss,
@@ -323,15 +326,20 @@
             sibling,
         )
 
+    param_refs = (taps_ref, bias_ref, gain_ref)
+
+    def param_dst(i):
+        return pk.at[x] if i == 0 else (pb, pg)[i - 1].at[x, 0]
+
     def p_send(i):
-        src = (taps_ref, bias_ref, gain_ref)[i]
-        dst = (pk, pb, pg)[i]
-        return remote(src, dst.at[x], p_ss.at[i], p_rs.at[i], x_peer)
+        return remote(param_refs[i], param_dst(i), p_ss.at[i], p_rs.at[i], x_peer)
 
     local_copies = (
         pltpu.make_async_copy(weight_ref, wbuf.at[x], local_sem.at[0]),
         pltpu.make_async_copy(frames_ref.at[0], frames, local_sem.at[1]),
         pltpu.make_async_copy(cot_ref.at[0], cot, local_sem.at[2]),
+    ) + tuple(
+        pltpu.make_async_copy(param_refs[i], param_dst(i), local_sem.at[3 + i]) for i in range(3)
     )
 
     barrier = pltpu.get_barrier_semaphore()
@@ -352,9 +360,6 @@
             qkv_own(p, a).start()
     for copy in local_copies:
         copy.start()
-    pk[x] = taps_ref[...]
-    pb[x] = bias_ref[...]
-    pg[x] = gain_ref[...]
 
     valid_len = len_ref[0]
     keys = nz * rows
@@ -369,20 +374,19 @@
     def attend(p, off):
         zq = lax.rem(z + off, nz)
         query = qkv[p, 0, pl.ds(pl.multiple_of(zq * rows, rows), rows), :]
-        pieces = []
-        for head in range(2):
-            keep = low_lanes if head == 0 else jnp.logical_not(low_lanes)
-            one = jnp.where(keep, query, jnp.zeros_like(query))
-            scores = lax.dot_general(
-                one, qkv[p, 1], (((1,), (1,)), ((), ())), preferred_element_type=f32
-            )
-            scores = scores + key_fill
-            top = jnp.max(scores, axis=1, keepdims=True)
-            weights = jnp.exp((scores - top) * (1.0 / math.sqrt(HD)))
-            total = jnp.sum(weights, axis=1, keepdims=True)
-            summed = jnp.dot(weights.astype(bf16), qkv[p, 2], preferred_element_type=f32)
-            pieces.append(summed / total)
-        return jnp.where(low_lanes, pieces[0], pieces[1]).astype(bf16)
+        blank = jnp.zeros_like(query)
+        both = jnp.concatenate(
+            [jnp.where(low_lanes, query, blank), jnp.where(low_lanes, blank, query)], axis=0
+        )
+        scores = lax.dot_general(
+            both, qkv[p, 1], (((1,), (1,)), ((), ())), preferred_element_type=f32
+        )
+        scores = scores + key_fill
+        top = jnp.max(scores, axis=1, keepdims=True)
+        weights = jnp.exp((scores - top) * (1.0 / math.sqrt(HD)))
+        total = jnp.sum(weights, axis=1, keepdims=True)
+        summed = jnp.dot(weights.astype(bf16), qkv[p, 2], preferred_element_type=f32) / total
+        return jnp.where(low_lanes, summed[0:rows], summed[rows:]).astype(bf16)
 
     def attend_part(p):
         for a in range(3):
@@ -414,6 +418,8 @@
                     proj[h * half + t] += piece
 
     attend_part(0)
+    for copy in local_copies:
+        copy.wait()
     for i in range(3):
         p_send(i).wait_recv()
     n_taps = pk.shape[1]
@@ -428,8 +434,6 @@
         attend_part(p)
     w_send(parts - 1).wait_recv()
     w_forward(parts - 1).start()
-    for copy in local_copies:
-        copy.wait()
     for p in range(parts):
         project(p)
 
@@ -459,7 +463,7 @@
 
         @pl.when(z == 0)
         def _():
-            recv[0] = jnp.zeros(recv.shape[1:], recv.dtype)
+            recv[0] = jnp.zeros((recv.shape[1], EDGE, LANES), recv.dtype)
 
         @pl.when(z < nz - 1)
         def _():
@@ -467,7 +471,7 @@
 
         @pl.when(z == nz - 1)
         def _():
-            recv[1] = jnp.zeros(recv.shape[1:], recv.dtype)
+            recv[1] = jnp.zeros((recv.shape[1], EDGE, LANES), recv.dtype)
 
     def edges_wait(send, recv, ss, rs):
         up, down = edge_copies(send, recv, ss, rs)
@@ -530,9 +534,6 @@
         gsend[1, t] = grad_pre[rows - EDGE : rows].astype(bf16)
         return carry
 
-    lax.fori_loop(0, tiles, forward, 0)
-    edges_start(gsend, grecv, g_ss, g_rs)
-
     def tap_sums(t, carry):
         grad_pre = gext[t, EDGE : EDGE + rows, :]
         for r in range(8):
@@ -547,14 +548,45 @@
         mb[t] = mf[t].astype(bf16)
         return carry
 
-    lax.fori_loop(0, tiles, tap_sums, 0)
+    def forward_half(h):
+        def one(t, carry):
+            forward(t, carry)
+            return tap_sums(t, carry)
+
+        lax.fori_loop(h * half, h * half + half, one, 0)
+
+    def g_edges(h, k):
+        part = pl.ds(h * half, half)
+        return (
+            gsend.at[:, part],
+            grecv.at[:, part],
+            g_ss.at[k],
+            g_rs.at[k],
+        )
+
+    def g_fill(h):
+        def one(t, carry):
+            gext[t, 0:EDGE, :] = grecv[0, t].astype(f32)
+            gext[t, EDGE + rows : ext, :] = grecv[1, t].astype(f32)
+            return carry
+
+        lax.fori_loop(h * half, h * half + half, one, 0)
+
+    forward_half(1 - x)
     to_x = remote(mb.at[pl.ds((1 - x) * half, half)], abuf, r_ss.at[0], r_rs.at[0], x_peer)
     to_x.start()
-
-    edges_wait(gsend, grecv, g_ss, g_rs)
-    for t in range(tiles):
-        gext[t, 0:EDGE, :] = grecv[0, t].astype(f32)
-        gext[t, EDGE + rows : ext, :] = grecv[1, t].astype(f32)
+    edges_start(*g_edges(1 - x, 0))
+    forward_half(x)
+    block_copy = pltpu.make_async_copy(block_ref, block_out, local_sem.at[6])
+    block_copy.start()
+    edges_start(*g_edges(x, 1))
+    to_x.wait()
+    rs1[...] = mf[pl.ds(x * half, half)] + abuf[...].astype(f32)
+    bsend[...] = rs1[pl.ds((1 - c) * quarter, quarter)].astype(bf16)
+    to_core = remote(bsend, bbuf, r_ss.at[1], r_rs.at[1], sibling)
+    to_core.start()
+    edges_wait(*g_edges(1 - x, 0))
+    g_fill(1 - x)
     sums[...] = jnp.zeros(sums.shape, f32)
 
     def backward(t, carry):
@@ -565,15 +597,10 @@
         sums[1] += acc * nl[t, EDGE : EDGE + rows, :]
         return carry
 
-    lax.fori_loop(0, half, backward, 0)
-
-    to_x.wait()
-    rs1[...] = mf[pl.ds(x * half, half)] + abuf[...].astype(f32)
-    bsend[...] = rs1[pl.ds((1 - c) * quarter, quarter)].astype(bf16)
-    to_core = remote(bsend, bbuf, r_ss.at[1], r_rs.at[1], sibling)
-    to_core.start()
-
-    lax.fori_loop(half, tiles, backward, 0)
+    def backward_half(h):
+        lax.fori_loop(h * half, h * half + half, backward, 0)
+
+    backward_half(1 - x)
 
     to_core.wait()
     zbuf[z] = (rs1[pl.ds(c * quarter, quarter)] + bbuf[...].astype(f32)).astype(bf16)
@@ -590,6 +617,10 @@
     for off in range(1, nz):
         z_send(off).start()
 
+    edges_wait(*g_edges(x, 1))
+    g_fill(x)
+    backward_half(x)
+
     first_mean = jnp.sum(sums[0], axis=1, keepdims=True) * (1.0 / feats)
     second_mean = jnp.sum(sums[1], axis=1, keepdims=True) * (1.0 / feats)
 
@@ -600,6 +631,8 @@
         return carry
 
     lax.fori_loop(0, tiles, finish_grad, 0)
+    hgrad_copy = pltpu.make_async_copy(hgrad_ref, hgrad_out, local_sem.at[7])
+    hgrad_copy.start()
 
     for off in range(1, nz):
         z_send(off).wait()
@@ -621,14 +654,31 @@
     for i in range(3):
         p_send(i).wait_send()
 
+    block_copy.wait()
+    hgrad_copy.wait()
     back.wait()
     factor = 1.0 / math.sqrt(4 * rows * nz)
     for t in range(half):
         cols = slice(t * LANES, (t + 1) * LANES)
         taps_sum = tot[t, 0:n_taps, :] * factor
-        gk_ref[:, cols] = taps_sum * gain_ref[:, cols]
+        gk_ref[:, cols] = taps_sum * pg[x, :, cols]
         gb_ref[:, cols] = tot[t, n_taps : n_taps + 1, :] * factor
-        gg_ref[:, cols] = jnp.sum(taps_sum * taps_ref[:, cols], axis=0, keepdims=True)
+        gg_ref[:, cols] = jnp.sum(taps_sum * pk[x, :, cols], axis=0, keepdims=True)
+
+
+def deliver(block, hgrad, gk, gb, gg, block_out, hgrad_out, gk_out, gb_out, gg_out, sems):
+    pairs = (
+        (block, block_out.at[0]),
+        (hgrad, hgrad_out.at[0]),
+        (gk, gk_out),
+        (gb.at[0], gb_out),
+        (gg.at[0], gg_out),
+    )
+    copies = [pltpu.make_async_copy(src, dst, sems.at[i]) for i, (src, dst) in enumerate(pairs)]
+    for copy in copies:
+        copy.start()
+    for copy in copies:
+        copy.wait()
 
 
 def fused_shards(
@@ -685,7 +735,9 @@
         vmem((quarter, taps + 1, LANES), bf16),
         vmem((nz, quarter, taps + 1, LANES), bf16),
         vmem((half, taps + 1, LANES), f32),
-        dma((3,)),
+        vmem((rows, feats), bf16),
+        vmem((rows, feats), bf16),
+        dma((8,)),
         dma((parts, 3)),
         dma((parts, 3, nz - 1)),
         dma((parts, 3, nz - 1)),
@@ -700,15 +752,15 @@
         dma((3,)),
         dma((2,)),
         dma((2,)),
-        dma((2,)),
-        dma((2,)),
+        dma((2, 2)),
+        dma((2, 2)),
         dma((3,)),
         dma((3,)),
         dma((nz - 1,)),
         dma((nz - 1,)),
     ]
     here = pl.BlockSpec(memory_space=pltpu.VMEM)
-    there = pl.BlockSpec(memory_space=pl.ANY)
+    there = pl.BlockSpec(memory_space=pltpu.HBM)
     block_out, hidden_grad, grad_kernel, grad_bias, grad_gain = pl.pallas_call(
         functools.partial(fused_kernel, nz),
         out_shape=(
@@ -725,15 +777,15 @@
             pl.BlockSpec(memory_space=pltpu.SMEM),
             there,
             there,
-            here,
-            here,
-            here,
+            there,
+            there,
+            there,
             there,
         ],
-        out_specs=(here,) * 5,
+        out_specs=(there, there, here, here, here),
         scratch_shapes=scratch,
         compiler_params=pltpu.CompilerParams(
-            collective_id=0, has_side_effects=True, vmem_limit_bytes=40 * 1024 * 1024
+            collective_id=0, has_side_effects=True, vmem_limit_bytes=VMEM_GRANT
         ),
         name="conformer_window",
     )(
@@ -744,11 +796,27 @@
         frames_in,
         out_weight,
         conv_kernel,
-        conv_bias[None],
-        ln_gain[None],
+        conv_bias,
+        ln_gain,
         cotangent,
     )
-    return (block_out[None], hidden_grad[None], grad_kernel, grad_bias[0], grad_gain[0])
+    results = (block_out, hidden_grad, grad_kernel, grad_bias, grad_gain)
+    block_out, hidden_grad, grad_kernel, grad_bias, grad_gain = pl.pallas_call(
+        deliver,
+        out_shape=(
+            jax.ShapeDtypeStruct((1, rows, feats), bf16),
+            jax.ShapeDtypeStruct((1, rows, feats), bf16),
+            jax.ShapeDtypeStruct((taps, cols), f32),
+            jax.ShapeDtypeStruct((cols,), f32),
+            jax.ShapeDtypeStruct((cols,), f32),
+        ),
+        in_specs=[pl.BlockSpec(memory_space=pl.ANY)] * 5,
+        out_specs=(there,) * 5,
+        scratch_shapes=[dma((5,))],
+        compiler_params=pltpu.CompilerParams(vmem_limit_bytes=VMEM_GRANT),
+        name="deliver_results",
+    )(*results)
+    return (block_out, hidden_grad, grad_kernel, grad_bias, grad_gain)
 
 
 def shards_any(*args):

time: 63.3 us -> 77 us (1.22)
  Pallas kernels: 49.7 us -> 75.6 us
  local copies, waits for them, and re-layouts: 10.6 us -> 0 us
  other arithmetic: 1.21 us -> 0 us
    pallas_call x0 -> x1, Pallas kernels: none -> 28.1 us  [fused_shards(): pl.pallas_call(deliver, out_shape=(jax.ShapeDtypeStruct((1, rows, feats),...]
    unnamed x17 -> x0, local copies, waits for them, and re-layouts: 9.27 us -> none
    pallas_call x1, Pallas kernels: 49.7 us -> 47.5 us  [fused_shards(): pl.pallas_call(functools.partial(fused_kernel, nz), out_shape=(jax.ShapeD...]
    broadcast_in_dim x2 -> x0, local copies, waits for them, and re-layouts: 1.38 us -> none  [the longest x1 0.69 us: fused_shards(): conv_bias[None]]
    pallas_call x2 -> x0, other arithmetic: 1.21 us -> none  [fused_shards(): pl.pallas_call(functools.partial(fused_kernel, nz), out_shape=(jax.ShapeD...]
where the time goes in v2:
time: 77 us; the launch traced here: 76.9 us
  Pallas kernels  75.6 us (98%)
  between operations  1.29 us (2%)
    pallas_call x1, Pallas kernels, fused_shards(): pl.pallas_call(functools.partial(fused_kernel, nz), out_shape=(jax.ShapeD...  47.5 us
    pallas_call x1, Pallas kernels, fused_shards(): pl.pallas_call(deliver, out_shape=(jax.ShapeDtypeStruct((1, rows, feats),...  28.1 us

profile of v2, /device:TPU:0, one launch (start us, length us, event | category | flops | bytes accessed | tf_op | source)
XLA Modules:
  0.0 76.9 jit_solution(11871927279334505275)
XLA Ops:
  1.3 47.5 %conformer_window.1 = (bf16[128,1536]{1,0:T(8,128)(2,1)}, bf16[128,1536]{1,0:T(8,128)(2,1)}, f32[31,768]{1,0:T(8,128)}, f32[1,768]{1,0:T(1,128)}, f32[1,768]{1,0:T(1,128)}) custom-call(bf16[1,128,1024]{2,1,0:T(8,128)(2,1)} %q_ref.1, bf16[1,128,1024]{2,1,0:T(8,128)(2,1)} %k_ref.1, bf16[1,128,1024]{2,1,0:T(8,128)(2,1)} %v_ref.1, s32[1]{0:T(128)S(6)} %copy.15.len_ref, ...), custom_call_target="tpu_custom_call" | custom-call | tf_op jit(solution)/shard_map/conformer_window/pallas_call | solution.py:764
  48.7 28.1 %deliver_results.1 = (bf16[1,128,1536]{2,1,0:T(8,128)(2,1)}, bf16[1,128,1536]{2,1,0:T(8,128)(2,1)}, f32[31,768]{1,0:T(8,128)}, f32[768]{0:T(1024)}, f32[768]{0:T(1024)}) custom-call(bf16[128,1536]{1,0:T(8,128)(2,1)} %get-tuple-element.10.block, bf16[128,1536]{1,0:T(8,128)(2,1)} %get-tuple-element.11.hgrad, f32[31,768]{1,0:T(8,128)} %get-tuple-element.12.gk, ...), custom_call_target="tpu_custom_call" | custom-call | tf_op jit(solution)/shard_map/deliver_results/pallas_call | solution.py:804

commit v3 on v2

--- a/solution.py
+++ b/solution.py
@@ -226,6 +226,9 @@
     tot,
     block_ref,
     hgrad_ref,
+    wins,
+    pweights,
+    pscale,
     local_sem,
     qkv_local,
     qkv_ss,
@@ -348,10 +351,10 @@
         pl.semaphore_signal(barrier, inc=1, device_id=dev, device_id_type=MESH)
     pl.semaphore_wait(barrier, len(partners))
 
+    for a in range(3):
+        for off in range(1, nz):
+            qkv_send(0, a, off).start()
     for p in range(parts):
-        for a in range(3):
-            for off in range(1, nz):
-                qkv_send(p, a, off).start()
         w_send(p).start()
         if p == 0:
             for i in range(3):
@@ -371,7 +374,7 @@
     positions = z * rows - EDGE + lax.broadcasted_iota(jnp.int32, (ext, LANES), 0)
     live[...] = jnp.where((positions >= 0) & (positions < valid_len), 1.0, 0.0).astype(f32)
 
-    def attend(p, off):
+    def score_chunk(p, off):
         zq = lax.rem(z + off, nz)
         query = qkv[p, 0, pl.ds(pl.multiple_of(zq * rows, rows), rows), :]
         blank = jnp.zeros_like(query)
@@ -385,22 +388,31 @@
         top = jnp.max(scores, axis=1, keepdims=True)
         weights = jnp.exp((scores - top) * (1.0 / math.sqrt(HD)))
         total = jnp.sum(weights, axis=1, keepdims=True)
-        summed = jnp.dot(weights.astype(bf16), qkv[p, 2], preferred_element_type=f32) / total
+        pweights[off] = weights.astype(bf16)
+        pscale[off] = jnp.broadcast_to(total, (2 * rows, LANES))
+
+    def value_chunk(p, off):
+        summed = jnp.dot(pweights[off], qkv[p, 2], preferred_element_type=f32) / pscale[off]
         return jnp.where(low_lanes, summed[0:rows], summed[rows:]).astype(bf16)
 
+    def arrived(p, a):
+        qkv_own(p, a).wait()
+        for off in range(1, nz):
+            qkv_send(p, a, off).wait_recv()
+        if p + 1 < parts:
+            for off in range(1, nz):
+                qkv_send(p + 1, a, off).start()
+
     def attend_part(p):
-        for a in range(3):
-            qkv_own(p, a).wait()
-            for off in range(1, nz):
-                qkv_send(p, a, off).wait_recv()
-
-        def one_chunk(i, carry):
-            osend[p, i] = attend(p, i + 1)
-            o_send(p, i + 1).start()
-            return carry
-
-        lax.fori_loop(0, nz - 1, one_chunk, 0)
-        obuf[p, :, pl.ds(pl.multiple_of(z * LANES, LANES), LANES)] = attend(p, 0)
+        arrived(p, 0)
+        arrived(p, 1)
+        for off in range(nz):
+            score_chunk(p, off)
+        arrived(p, 2)
+        for off in range(1, nz):
+            osend[p, off - 1] = value_chunk(p, off)
+            o_send(p, off).start()
+        obuf[p, :, pl.ds(pl.multiple_of(z * LANES, LANES), LANES)] = value_chunk(p, 0)
 
     def project(p):
         for off in range(1, nz):
@@ -510,9 +522,12 @@
     norm_rows(0, EDGE)
     norm_rows(EDGE + rows, EDGE)
 
-    def shifted_sum(acc, source, t, flip):
+    def shifted_sum(acc, source, t, flip, keep=None):
+        whole = source[t]
         for r in range(8):
-            window = source[t, r : r + rows + 24, :]
+            window = whole if r == 0 else pltpu.roll(whole, ext - r, 0)
+            if keep is not None:
+                keep[r] = window
             for a in range(4):
                 shift = 8 * a + r
                 tap = n_taps - shift if flip else shift - 1
@@ -522,7 +537,7 @@
 
     def forward(t, carry):
         start = jnp.broadcast_to(kp[t, n_taps : n_taps + 1, :], (rows, LANES))
-        pre = shifted_sum(start, nl, t, False)
+        pre = shifted_sum(start, nl, t, False, wins)
         alive = live[EDGE : EDGE + rows, :]
         gate = 1.0 / (1.0 + jnp.exp(-pre))
         hidden = hid[t, EDGE : EDGE + rows, :]
@@ -537,12 +552,11 @@
     def tap_sums(t, carry):
         grad_pre = gext[t, EDGE : EDGE + rows, :]
         for r in range(8):
-            window = nl[t, r : r + rows + 24, :]
             for a in range(4):
                 shift = 8 * a + r
                 if shift > 0:
                     mf[t, shift - 1 : shift, :] = jnp.sum(
-                        grad_pre * window[8 * a : 8 * a + rows], axis=0, keepdims=True
+                        grad_pre * wins[r, 8 * a : 8 * a + rows, :], axis=0, keepdims=True
                     )
         mf[t, n_taps : n_taps + 1, :] = jnp.sum(grad_pre, axis=0, keepdims=True)
         mb[t] = mf[t].astype(bf16)
@@ -666,19 +680,19 @@
         gg_ref[:, cols] = jnp.sum(taps_sum * pk[x, :, cols], axis=0, keepdims=True)
 
 
-def deliver(block, hgrad, gk, gb, gg, block_out, hgrad_out, gk_out, gb_out, gg_out, sems):
-    pairs = (
-        (block, block_out.at[0]),
-        (hgrad, hgrad_out.at[0]),
-        (gk, gk_out),
-        (gb.at[0], gb_out),
-        (gg.at[0], gg_out),
-    )
-    copies = [pltpu.make_async_copy(src, dst, sems.at[i]) for i, (src, dst) in enumerate(pairs)]
-    for copy in copies:
-        copy.start()
-    for copy in copies:
-        copy.wait()
+def deliver(*refs):
+    ins, outs, held, sem_in, sem_out = refs[0:5], refs[5:10], refs[10:15], refs[15], refs[16]
+    targets = (outs[0].at[0], outs[1].at[0], outs[2], outs[3], outs[4])
+    sources = (held[0], held[1], held[2], held[3].at[0], held[4].at[0])
+    reads = [pltpu.make_async_copy(ins[i], held[i], sem_in.at[i]) for i in range(5)]
+    writes = [pltpu.make_async_copy(sources[i], targets[i], sem_out.at[i]) for i in range(5)]
+    for read in reads:
+        read.start()
+    for read, write in zip(reads, writes):
+        read.wait()
+        write.start()
+    for write in writes:
+        write.wait()
 
 
 def fused_shards(
@@ -737,6 +751,9 @@
         vmem((half, taps + 1, LANES), f32),
         vmem((rows, feats), bf16),
         vmem((rows, feats), bf16),
+        vmem((8, ext, LANES), f32),
+        vmem((nz, 2 * rows, nz * rows), bf16),
+        vmem((nz, 2 * rows, LANES), f32),
         dma((8,)),
         dma((parts, 3)),
         dma((parts, 3, nz - 1)),
@@ -812,7 +829,7 @@
         ),
         in_specs=[pl.BlockSpec(memory_space=pl.ANY)] * 5,
         out_specs=(there,) * 5,
-        scratch_shapes=[dma((5,))],
+        scratch_shapes=[vmem(value.shape, value.dtype) for value in results] + [dma((5,)), dma((5,))],
         compiler_params=pltpu.CompilerParams(vmem_limit_bytes=VMEM_GRANT),
         name="deliver_results",
     )(*results)

time: 77 us -> 51.9 us (0.67)
  Pallas kernels: 75.6 us -> 50.4 us
    pallas_call x1, Pallas kernels: 28.1 us -> 1.99 us  [fused_shards(): pl.pallas_call(deliver, out_shape=(jax.ShapeDtypeStruct((1, rows, feats),...]
    pallas_call x1, Pallas kernels: 47.5 us -> 48.4 us  [fused_shards(): pl.pallas_call(functools.partial(fused_kernel, nz), out_shape=(jax.ShapeD...]
where the time goes in v3:
time: 51.9 us; the launch traced here: 51.7 us
  Pallas kernels  50.4 us (97%)
  between operations  1.29 us (2%)
    pallas_call x1, Pallas kernels, fused_shards(): pl.pallas_call(functools.partial(fused_kernel, nz), out_shape=(jax.ShapeD...  48.4 us
    pallas_call x1, Pallas kernels, fused_shards(): pl.pallas_call(deliver, out_shape=(jax.ShapeDtypeStruct((1, rows, feats),...  1.99 us

profile of v3, /device:TPU:0, one launch (start us, length us, event | category | flops | bytes accessed | tf_op | source)
XLA Modules:
  0.0 51.7 jit_solution(6842575032511111186)
XLA Ops:
  1.3 48.4 %conformer_window.1 = (bf16[128,1536]{1,0:T(8,128)(2,1)}, bf16[128,1536]{1,0:T(8,128)(2,1)}, f32[31,768]{1,0:T(8,128)}, f32[1,768]{1,0:T(1,128)}, f32[1,768]{1,0:T(1,128)}) custom-call(bf16[1,128,1024]{2,1,0:T(8,128)(2,1)} %q_ref.1, bf16[1,128,1024]{2,1,0:T(8,128)(2,1)} %k_ref.1, bf16[1,128,1024]{2,1,0:T(8,128)(2,1)} %v_ref.1, s32[1]{0:T(128)S(6)} %copy.15.len_ref, ...), custom_call_target="tpu_custom_call" | custom-call | tf_op jit(solution)/shard_map/conformer_window/pallas_call | solution.py:781
  49.7 2.0 %deliver_results.1 = (bf16[1,128,1536]{2,1,0:T(8,128)(2,1)}, bf16[1,128,1536]{2,1,0:T(8,128)(2,1)}, f32[31,768]{1,0:T(8,128)}, f32[768]{0:T(1024)}, f32[768]{0:T(1024)}) custom-call(bf16[128,1536]{1,0:T(8,128)(2,1)} %get-tuple-element.10.refs_0_, bf16[128,1536]{1,0:T(8,128)(2,1)} %get-tuple-element.11.refs_1_, f32[31,768]{1,0:T(8,128)} %get-tuple-element.12.refs_2_, ...), custom_call_target="tpu_custom_call" | custom-call | tf_op jit(solution)/shard_map/deliver_results/pallas_call | solution.py:821

commit v4 on v3

--- a/solution.py
+++ b/solution.py
@@ -262,6 +262,7 @@
     tiles = proj.shape[0]
     half = tiles // 2
     quarter = half // 2
+    unroll = 3 if half % 3 == 0 else 1
     wrows = wbuf.shape[1] // parts // 2
     feats = tiles * LANES
 
@@ -355,12 +356,11 @@
         for off in range(1, nz):
             qkv_send(0, a, off).start()
     for p in range(parts):
-        w_send(p).start()
-        if p == 0:
-            for i in range(3):
-                p_send(i).start()
         for a in range(3):
             qkv_own(p, a).start()
+    w_send(0).start()
+    for i in range(3):
+        p_send(i).start()
     for copy in local_copies:
         copy.start()
 
@@ -402,6 +402,8 @@
         if p + 1 < parts:
             for off in range(1, nz):
                 qkv_send(p + 1, a, off).start()
+            if a == 2:
+                w_send(p + 1).start()
 
     def attend_part(p):
         arrived(p, 0)
@@ -424,10 +426,17 @@
             product = jnp.dot(attended, block, preferred_element_type=f32)
             for t in range(half):
                 piece = product[:, t * LANES : (t + 1) * LANES]
-                if p == 0:
-                    proj[h * half + t] = piece
+                tile = h * half + t
+                if p > 0:
+                    piece = piece + proj[tile]
+                if p < parts - 1:
+                    proj[tile] = piece
                 else:
-                    proj[h * half + t] += piece
+                    frame = frames[:, tile * LANES : (tile + 1) * LANES].astype(f32)
+                    value = (frame + piece).astype(bf16)
+                    hsend[0, tile] = value[0:EDGE]
+                    hsend[1, tile] = value[rows - EDGE : rows]
+                    hid[tile, EDGE : EDGE + rows, :] = value.astype(f32)
 
     attend_part(0)
     for copy in local_copies:
@@ -452,15 +461,6 @@
     def lane_cols(t):
         return pl.ds(pl.multiple_of(t * LANES, LANES), LANES)
 
-    def finish_hidden(t, carry):
-        value = (frames[:, lane_cols(t)].astype(f32) + proj[t]).astype(bf16)
-        hsend[0, t] = value[0:EDGE]
-        hsend[1, t] = value[rows - EDGE : rows]
-        hid[t, EDGE : EDGE + rows, :] = value.astype(f32)
-        return carry
-
-    lax.fori_loop(0, tiles, finish_hidden, 0)
-
     def edge_copies(send, recv, ss, rs):
         up = remote(send.at[0], recv.at[1], ss.at[0], rs.at[1], at_z(lax.rem(z + nz - 1, nz)))
         down = remote(send.at[1], recv.at[0], ss.at[1], rs.at[0], at_z(lax.rem(z + 1, nz)))
@@ -498,29 +498,40 @@
             down.wait_send()
             up.wait_recv()
 
-    def norm_rows(start, count):
-        total = jnp.zeros((count, LANES), f32)
+    def norm_rows(load, alive, store):
+        total = load(0)
+        for t in range(1, tiles):
+            total = total + load(t)
+        mean = jnp.sum(total, axis=1, keepdims=True) * (1.0 / feats)
+        total = jnp.zeros(total.shape, f32)
         for t in range(tiles):
-            total = total + hid[t, start : start + count, :]
-        mean = jnp.sum(total, axis=1, keepdims=True) * (1.0 / feats)
-        total = jnp.zeros((count, LANES), f32)
-        for t in range(tiles):
-            centered = hid[t, start : start + count, :] - mean
+            centered = load(t) - mean
             total = total + centered * centered
         inv = lax.rsqrt(jnp.sum(total, axis=1, keepdims=True) * (1.0 / feats) + 1e-05)
-        scale = live[start : start + count, :] * inv
+        scale = alive * inv
         for t in range(tiles):
-            nl[t, start : start + count, :] = (hid[t, start : start + count, :] - mean) * scale
+            store(t, (load(t) - mean) * scale)
         return inv
 
+    def load_own(t):
+        return hid[t, EDGE : EDGE + rows, :]
+
+    def store_own(t, value):
+        nl[t, EDGE : EDGE + rows, :] = value
+
+    def load_edges(t):
+        return jnp.concatenate([hrecv[0, t], hrecv[1, t]], axis=0).astype(f32)
+
+    def store_edges(t, value):
+        nl[t, 0:EDGE, :] = value[0:EDGE]
+        nl[t, EDGE + rows : ext, :] = value[EDGE:]
+
     edges_start(hsend, hrecv, h_ss, h_rs)
-    invs[...] = jnp.broadcast_to(norm_rows(EDGE, rows), (rows, LANES))
+    inv_own = norm_rows(load_own, live[EDGE : EDGE + rows, :], store_own)
+    invs[...] = jnp.broadcast_to(inv_own, (rows, LANES))
     edges_wait(hsend, hrecv, h_ss, h_rs)
-    for t in range(tiles):
-        hid[t, 0:EDGE, :] = hrecv[0, t].astype(f32)
-        hid[t, EDGE + rows : ext, :] = hrecv[1, t].astype(f32)
-    norm_rows(0, EDGE)
-    norm_rows(EDGE + rows, EDGE)
+    live_edges = jnp.concatenate([live[0:EDGE, :], live[EDGE + rows : ext, :]], axis=0)
+    norm_rows(load_edges, live_edges, store_edges)
 
     def shifted_sum(acc, source, t, flip, keep=None):
         whole = source[t]
@@ -535,9 +546,9 @@
                     acc = acc + kp[t, tap : tap + 1, :] * window[8 * a : 8 * a + rows]
         return acc
 
-    def forward(t, carry):
+    def forward(t, carry, slot=0):
         start = jnp.broadcast_to(kp[t, n_taps : n_taps + 1, :], (rows, LANES))
-        pre = shifted_sum(start, nl, t, False, wins)
+        pre = shifted_sum(start, nl, t, False, wins.at[slot])
         alive = live[EDGE : EDGE + rows, :]
         gate = 1.0 / (1.0 + jnp.exp(-pre))
         hidden = hid[t, EDGE : EDGE + rows, :]
@@ -549,25 +560,36 @@
         gsend[1, t] = grad_pre[rows - EDGE : rows].astype(bf16)
         return carry
 
-    def tap_sums(t, carry):
+    def tap_sums(t, carry, slot=0):
         grad_pre = gext[t, EDGE : EDGE + rows, :]
         for r in range(8):
             for a in range(4):
                 shift = 8 * a + r
                 if shift > 0:
                     mf[t, shift - 1 : shift, :] = jnp.sum(
-                        grad_pre * wins[r, 8 * a : 8 * a + rows, :], axis=0, keepdims=True
+                        grad_pre * wins[slot, r, 8 * a : 8 * a + rows, :], axis=0, keepdims=True
                     )
         mf[t, n_taps : n_taps + 1, :] = jnp.sum(grad_pre, axis=0, keepdims=True)
         mb[t] = mf[t].astype(bf16)
         return carry
 
+    def over_half(h, body):
+        def step(i, carry):
+            for j in range(unroll):
+                body(h * half + i * unroll + j, 0)
+            return carry
+
+        lax.fori_loop(0, half // unroll, step, 0)
+
     def forward_half(h):
-        def one(t, carry):
-            forward(t, carry)
-            return tap_sums(t, carry)
-
-        lax.fori_loop(h * half, h * half + half, one, 0)
+        def step(i, carry):
+            for j in range(unroll):
+                forward(h * half + i * unroll + j, 0, j)
+            for j in range(unroll):
+                tap_sums(h * half + i * unroll + j, 0, j)
+            return carry
+
+        lax.fori_loop(0, half // unroll, step, 0)
 
     def g_edges(h, k):
         part = pl.ds(h * half, half)
@@ -584,7 +606,7 @@
             gext[t, EDGE + rows : ext, :] = grecv[1, t].astype(f32)
             return carry
 
-        lax.fori_loop(h * half, h * half + half, one, 0)
+        over_half(h, one)
 
     forward_half(1 - x)
     to_x = remote(mb.at[pl.ds((1 - x) * half, half)], abuf, r_ss.at[0], r_rs.at[0], x_peer)
@@ -612,7 +634,7 @@
         return carry
 
     def backward_half(h):
-        lax.fori_loop(h * half, h * half + half, backward, 0)
+        over_half(h, backward)
 
     backward_half(1 - x)
 
@@ -644,7 +666,8 @@
         hgrad_ref[:, lane_cols(t)] = value.astype(bf16)
         return carry
 
-    lax.fori_loop(0, tiles, finish_grad, 0)
+    over_half(0, finish_grad)
+    over_half(1, finish_grad)
     hgrad_copy = pltpu.make_async_copy(hgrad_ref, hgrad_out, local_sem.at[7])
     hgrad_copy.start()
 
@@ -751,7 +774,7 @@
         vmem((half, taps + 1, LANES), f32),
         vmem((rows, feats), bf16),
         vmem((rows, feats), bf16),
-        vmem((8, ext, LANES), f32),
+        vmem((3, 8, ext, LANES), f32),
         vmem((nz, 2 * rows, nz * rows), bf16),
         vmem((nz, 2 * rows, LANES), f32),
         dma((8,)),

time: 51.9 us -> 51.6 us (level)
  no operation moved by 1% of the time
where the time goes in v4:
time: 51.6 us; the launch traced here: 51.5 us
  Pallas kernels  50.2 us (97%)
  between operations  1.29 us (2%)
    pallas_call x1, Pallas kernels, fused_shards(): pl.pallas_call(functools.partial(fused_kernel, nz), out_shape=(jax.ShapeD...  48.2 us
    pallas_call x1, Pallas kernels, fused_shards(): pl.pallas_call(deliver, out_shape=(jax.ShapeDtypeStruct((1, rows, feats),...  1.99 us

profile of v4, /device:TPU:0, one launch (start us, length us, event | category | flops | bytes accessed | tf_op | source)
XLA Modules:
  0.0 51.5 jit_solution(13741969086199632446)
XLA Ops:
  1.3 48.2 %conformer_window.1 = (bf16[128,1536]{1,0:T(8,128)(2,1)}, bf16[128,1536]{1,0:T(8,128)(2,1)}, f32[31,768]{1,0:T(8,128)}, f32[1,768]{1,0:T(1,128)}, f32[1,768]{1,0:T(1,128)}) custom-call(bf16[1,128,1024]{2,1,0:T(8,128)(2,1)} %q_ref.1, bf16[1,128,1024]{2,1,0:T(8,128)(2,1)} %k_ref.1, bf16[1,128,1024]{2,1,0:T(8,128)(2,1)} %v_ref.1, s32[1]{0:T(128)S(6)} %copy.15.len_ref, ...), custom_call_target="tpu_custom_call" | custom-call | tf_op jit(solution)/shard_map/conformer_window/pallas_call | solution.py:804
  49.5 2.0 %deliver_results.1 = (bf16[1,128,1536]{2,1,0:T(8,128)(2,1)}, bf16[1,128,1536]{2,1,0:T(8,128)(2,1)}, f32[31,768]{1,0:T(8,128)}, f32[768]{0:T(1024)}, f32[768]{0:T(1024)}) custom-call(bf16[128,1536]{1,0:T(8,128)(2,1)} %get-tuple-element.10.refs_0_, bf16[128,1536]{1,0:T(8,128)(2,1)} %get-tuple-element.11.refs_1_, f32[31,768]{1,0:T(8,128)} %get-tuple-element.12.refs_2_, ...), custom_call_target="tpu_custom_call" | custom-call | tf_op jit(solution)/shard_map/deliver_results/pallas_call | solution.py:844

commit v5 on v4

--- a/solution.py
+++ b/solution.py
@@ -262,7 +262,7 @@
     tiles = proj.shape[0]
     half = tiles // 2
     quarter = half // 2
-    unroll = 3 if half % 3 == 0 else 1
+    unroll = 1
     wrows = wbuf.shape[1] // parts // 2
     feats = tiles * LANES
 
@@ -399,46 +399,38 @@
         qkv_own(p, a).wait()
         for off in range(1, nz):
             qkv_send(p, a, off).wait_recv()
-        if p + 1 < parts:
+
+        @pl.when(p + 1 < parts)
+        def _():
             for off in range(1, nz):
                 qkv_send(p + 1, a, off).start()
             if a == 2:
                 w_send(p + 1).start()
 
-    def attend_part(p):
+    def attend_part(p, carry):
         arrived(p, 0)
         arrived(p, 1)
-        for off in range(nz):
+
+        def one_score(off, inner):
             score_chunk(p, off)
+            return inner
+
+        lax.fori_loop(0, nz, one_score, 0)
         arrived(p, 2)
-        for off in range(1, nz):
+
+        def one_value(off, inner):
             osend[p, off - 1] = value_chunk(p, off)
             o_send(p, off).start()
+            return inner
+
+        lax.fori_loop(1, nz, one_value, 0)
         obuf[p, :, pl.ds(pl.multiple_of(z * LANES, LANES), LANES)] = value_chunk(p, 0)
-
-    def project(p):
-        for off in range(1, nz):
-            o_send(p, off).wait_recv()
-        w_forward(p).wait_recv()
-        attended = obuf[p]
-        for h in range(2):
-            block = wbuf[h, p * part_cols : (p + 1) * part_cols, :]
-            product = jnp.dot(attended, block, preferred_element_type=f32)
-            for t in range(half):
-                piece = product[:, t * LANES : (t + 1) * LANES]
-                tile = h * half + t
-                if p > 0:
-                    piece = piece + proj[tile]
-                if p < parts - 1:
-                    proj[tile] = piece
-                else:
-                    frame = frames[:, tile * LANES : (tile + 1) * LANES].astype(f32)
-                    value = (frame + piece).astype(bf16)
-                    hsend[0, tile] = value[0:EDGE]
-                    hsend[1, tile] = value[rows - EDGE : rows]
-                    hid[tile, EDGE : EDGE + rows, :] = value.astype(f32)
-
-    attend_part(0)
+        w_send(p).wait_recv()
+        w_forward(p).start()
+        return carry
+
+    lax.fori_loop(0, parts, attend_part, 0)
+
     for copy in local_copies:
         copy.wait()
     for i in range(3):
@@ -449,17 +441,41 @@
             cols = slice(t * LANES, (t + 1) * LANES)
             kp[h * half + t, 0:n_taps, :] = pk[h, :, cols] * pg[h, :, cols]
             kp[h * half + t, n_taps : n_taps + 1, :] = pb[h, :, cols]
-    for p in range(1, parts):
-        w_send(p - 1).wait_recv()
-        w_forward(p - 1).start()
-        attend_part(p)
-    w_send(parts - 1).wait_recv()
-    w_forward(parts - 1).start()
-    for p in range(parts):
-        project(p)
+
+    def first_hidden(t, carry):
+        proj[t] = frames[:, lane_cols(t)].astype(f32)
+        return carry
+
+    def project(p, carry):
+        for off in range(1, nz):
+            o_send(p, off).wait_recv()
+        w_forward(p).wait_recv()
+        depth = pl.ds(pl.multiple_of(p * part_cols, part_cols), part_cols)
+
+        def one_block(b, inner):
+            start = pl.multiple_of(lax.rem(b, quarter) * 2 * LANES, 2 * LANES)
+            block = wbuf[lax.div(b, quarter), depth, pl.ds(start, 2 * LANES)]
+            product = jnp.dot(obuf[p], block, preferred_element_type=f32)
+            proj[2 * b] += product[:, 0:LANES]
+            proj[2 * b + 1] += product[:, LANES:]
+            return inner
+
+        lax.fori_loop(0, half, one_block, 0)
+        return carry
+
+    def finish_hidden(t, carry):
+        value = proj[t].astype(bf16)
+        hsend[0, t] = value[0:EDGE]
+        hsend[1, t] = value[rows - EDGE : rows]
+        hid[t, EDGE : EDGE + rows, :] = value.astype(f32)
+        return carry
 
     def lane_cols(t):
         return pl.ds(pl.multiple_of(t * LANES, LANES), LANES)
+
+    lax.fori_loop(0, tiles, first_hidden, 0)
+    lax.fori_loop(0, parts, project, 0)
+    lax.fori_loop(0, tiles, finish_hidden, 0)
 
     def edge_copies(send, recv, ss, rs):
         up = remote(send.at[0], recv.at[1], ss.at[0], rs.at[1], at_z(lax.rem(z + nz - 1, nz)))
@@ -499,18 +515,23 @@
             up.wait_recv()
 
     def norm_rows(load, alive, store):
-        total = load(0)
-        for t in range(1, tiles):
-            total = total + load(t)
+        blank = jnp.zeros(alive.shape, f32)
+        total = lax.fori_loop(0, tiles, lambda t, acc: acc + load(t), blank, unroll=2)
         mean = jnp.sum(total, axis=1, keepdims=True) * (1.0 / feats)
-        total = jnp.zeros(total.shape, f32)
-        for t in range(tiles):
+
+        def add_square(t, acc):
             centered = load(t) - mean
-            total = total + centered * centered
+            return acc + centered * centered
+
+        total = lax.fori_loop(0, tiles, add_square, blank, unroll=2)
         inv = lax.rsqrt(jnp.sum(total, axis=1, keepdims=True) * (1.0 / feats) + 1e-05)
         scale = alive * inv
-        for t in range(tiles):
+
+        def put(t, carry):
             store(t, (load(t) - mean) * scale)
+            return carry
+
+        lax.fori_loop(0, tiles, put, 0, unroll=2)
         return inv
 
     def load_own(t):
@@ -774,7 +795,7 @@
         vmem((half, taps + 1, LANES), f32),
         vmem((rows, feats), bf16),
         vmem((rows, feats), bf16),
-        vmem((3, 8, ext, LANES), f32),
+        vmem((1, 8, ext, LANES), f32),
         vmem((nz, 2 * rows, nz * rows), bf16),
         vmem((nz, 2 * rows, LANES), f32),
         dma((8,)),

time: 51.6 us -> 52.7 us (1.021)
  Pallas kernels: 50.2 us -> 51.2 us
    pallas_call x1, Pallas kernels: 48.2 us -> 49.2 us  [fused_shards(): pl.pallas_call(functools.partial(fused_kernel, nz), out_shape=(jax.ShapeD...]
where the time goes in v5:
time: 52.7 us; the launch traced here: 52.5 us
  Pallas kernels  51.2 us (97%)
  between operations  1.29 us (2%)
    pallas_call x1, Pallas kernels, fused_shards(): pl.pallas_call(functools.partial(fused_kernel, nz), out_shape=(jax.ShapeD...  49.2 us
    pallas_call x1, Pallas kernels, fused_shards(): pl.pallas_call(deliver, out_shape=(jax.ShapeDtypeStruct((1, rows, feats),...  1.99 us

profile of v5, /device:TPU:0, one launch (start us, length us, event | category | flops | bytes accessed | tf_op | source)
XLA Modules:
  0.0 52.5 jit_solution(12463063156330431807)
XLA Ops:
  1.3 49.2 %conformer_window.1 = (bf16[128,1536]{1,0:T(8,128)(2,1)}, bf16[128,1536]{1,0:T(8,128)(2,1)}, f32[31,768]{1,0:T(8,128)}, f32[1,768]{1,0:T(1,128)}, f32[1,768]{1,0:T(1,128)}) custom-call(bf16[1,128,1024]{2,1,0:T(8,128)(2,1)} %q_ref.1, bf16[1,128,1024]{2,1,0:T(8,128)(2,1)} %k_ref.1, bf16[1,128,1024]{2,1,0:T(8,128)(2,1)} %v_ref.1, s32[1]{0:T(128)S(6)} %copy.15.len_ref, ...), custom_call_target="tpu_custom_call" | custom-call | tf_op jit(solution)/shard_map/conformer_window/pallas_call | solution.py:825
  50.5 2.0 %deliver_results.1 = (bf16[1,128,1536]{2,1,0:T(8,128)(2,1)}, bf16[1,128,1536]{2,1,0:T(8,128)(2,1)}, f32[31,768]{1,0:T(8,128)}, f32[768]{0:T(1024)}, f32[768]{0:T(1024)}) custom-call(bf16[128,1536]{1,0:T(8,128)(2,1)} %get-tuple-element.10.refs_0_, bf16[128,1536]{1,0:T(8,128)(2,1)} %get-tuple-element.11.refs_1_, f32[31,768]{1,0:T(8,128)} %get-tuple-element.12.refs_2_, ...), custom_call_target="tpu_custom_call" | custom-call | tf_op jit(solution)/shard_map/deliver_results/pallas_call | solution.py:865

commit v6 on v4

--- a/solution.py
+++ b/solution.py
@@ -352,15 +352,17 @@
         pl.semaphore_signal(barrier, inc=1, device_id=dev, device_id_type=MESH)
     pl.semaphore_wait(barrier, len(partners))
 
-    for a in range(3):
-        for off in range(1, nz):
-            qkv_send(0, a, off).start()
+    for p in range(parts):
+        for a in range(3):
+            for off in range(1, nz):
+                qkv_send(p, a, off).start()
+        w_send(p).start()
+        if p == 0:
+            for i in range(3):
+                p_send(i).start()
     for p in range(parts):
         for a in range(3):
             qkv_own(p, a).start()
-    w_send(0).start()
-    for i in range(3):
-        p_send(i).start()
     for copy in local_copies:
         copy.start()
 
@@ -399,11 +401,6 @@
         qkv_own(p, a).wait()
         for off in range(1, nz):
             qkv_send(p, a, off).wait_recv()
-        if p + 1 < parts:
-            for off in range(1, nz):
-                qkv_send(p + 1, a, off).start()
-            if a == 2:
-                w_send(p + 1).start()
 
     def attend_part(p):
         arrived(p, 0)

time: 51.6 us -> 50.4 us (0.977)
  Pallas kernels: 50.2 us -> 49 us
    pallas_call x1, Pallas kernels: 48.2 us -> 47 us  [fused_shards(): pl.pallas_call(functools.partial(fused_kernel, nz), out_shape=(jax.ShapeD...]
where the time goes in v6:
time: 50.4 us; the launch traced here: 50.2 us
  Pallas kernels  49 us (97%)
  between operations  1.29 us (3%)
    pallas_call x1, Pallas kernels, fused_shards(): pl.pallas_call(functools.partial(fused_kernel, nz), out_shape=(jax.ShapeD...  47 us
    pallas_call x1, Pallas kernels, fused_shards(): pl.pallas_call(deliver, out_shape=(jax.ShapeDtypeStruct((1, rows, feats),...  1.99 us

profile of v6, /device:TPU:0, one launch (start us, length us, event | category | flops | bytes accessed | tf_op | source)
XLA Modules:
  0.0 50.2 jit_solution(16048185464664430833)
XLA Ops:
  1.3 47.0 %conformer_window.1 = (bf16[128,1536]{1,0:T(8,128)(2,1)}, bf16[128,1536]{1,0:T(8,128)(2,1)}, f32[31,768]{1,0:T(8,128)}, f32[1,768]{1,0:T(1,128)}, f32[1,768]{1,0:T(1,128)}) custom-call(bf16[1,128,1024]{2,1,0:T(8,128)(2,1)} %q_ref.1, bf16[1,128,1024]{2,1,0:T(8,128)(2,1)} %k_ref.1, bf16[1,128,1024]{2,1,0:T(8,128)(2,1)} %v_ref.1, s32[1]{0:T(128)S(6)} %copy.15.len_ref, ...), custom_call_target="tpu_custom_call" | custom-call | tf_op jit(solution)/shard_map/conformer_window/pallas_call | solution.py:801
  48.3 2.0 %deliver_results.1 = (bf16[1,128,1536]{2,1,0:T(8,128)(2,1)}, bf16[1,128,1536]{2,1,0:T(8,128)(2,1)}, f32[31,768]{1,0:T(8,128)}, f32[768]{0:T(1024)}, f32[768]{0:T(1024)}) custom-call(bf16[128,1536]{1,0:T(8,128)(2,1)} %get-tuple-element.10.refs_0_, bf16[128,1536]{1,0:T(8,128)(2,1)} %get-tuple-element.11.refs_1_, f32[31,768]{1,0:T(8,128)} %get-tuple-element.12.refs_2_, ...), custom_call_target="tpu_custom_call" | custom-call | tf_op jit(solution)/shard_map/deliver_results/pallas_call | solution.py:841
